TPU v7x, 256 devices: a whole 4x4x8 slice. The times are simulated.
256 devices in a mesh: row: 32 (over z, y_lo, core), col: 8 (over x, y_hi).
Axes of the slice: x: 4, y: 4 (y_hi: 2, y_lo: 2; y = y_hi * 2 + y_lo), z: 8, core: 2. Of those that a mesh axis runs over, the one named last changes fastest.
Arguments:
- charges: bfloat16 [64, 1048576], P(None, ('row', 'col')), may hold values from -6 to 6
- points: float32 [3, 1048576], P(None, ('row', 'col')), may hold values from 0 to 128, as said below
- leaf_basis: bfloat16 [32, 1048576], P(None, ('row', 'col')), may hold values from -0.75 to 0.75
- transfer_one: bfloat16 [16384, 32, 32], P(('row', 'col')), may hold values from -0.5 to 0.5
- transfer_two: bfloat16 [2048, 32, 32], P(('row', 'col')), may hold values from -0.5 to 0.5
- couple_one: bfloat16 [2048, 12, 32, 32], P(('row', 'col')), may hold values from -0.3125 to 0.3125
- couple_two: bfloat16 [256, 16, 32, 32], P(('row', 'col')), may hold values from -0.25 to 0.25
- near_list: int32 [16384, 27], P(('row', 'col')), may hold values from -1 to 16383, as said below
- list_one: int32 [2048, 12], P(('row', 'col')), may hold values from -1 to 2047, as said below
- list_two: int32 [256, 16], P(('row', 'col')), may hold values from 0 to 255
Outputs:
- potential: bfloat16 [64, 1048576], P(None, ('row', 'col'))
Inputs may be any that keep to these rules, and one draw needn't show every extreme that they name: `points`: point p of the leaf at grid position (x, y, z) lies in the unit cube [x, x + 1) x [y, y + 1) x [z, z + 1). `near_list`: slot s = 9 (dz + 1) + 3 (dy + 1) + (dx + 1), with dx, dy, dz in -1, 0, 1, names the leaf at grid offset (dx, dy, dz) from the row's leaf, or is -1; it is -1 wherever that position lies outside the grid; slot 13 names the leaf itself. `list_one`: in each row the named nodes come first and the -1 entries last, at least 6 named; each named node has the same index // 64 as the row's node.
All inputs are finite; a program needn't handle non-finite values.
Results may differ from a plain program's by a relative error of at most 0.0053.
Values may be sent and summed in bfloat16 or wider, within the bound.
A program may use at most 128 MiB of HBM per device.

v0:
```python
import jax
import jax.numpy as jnp
from jax import lax
from jax.sharding import PartitionSpec as P

PTS = 64
BX = 4
BY = 4
NEAR = 27


softening = 0.0025


def padded(value, sides, width):
    for axis, dim in sides:
        devices, length = (lax.axis_size(axis), value.shape[dim])
        up = [(i, (i + 1) % devices) for i in range(devices - 1)]
        down = [(j, i) for i, j in up]
        last = lax.slice_in_dim(value, length - width, length, axis=dim)
        initial = lax.slice_in_dim(value, 0, width, axis=dim)
        before = lax.ppermute(last, axis, up)
        after = lax.ppermute(initial, axis, down)
        value = jnp.concatenate([before, value, after], axis=dim)
    return value


def laid_out(parts, dim):
    parts = jnp.moveaxis(parts, 0, dim)
    lengths = parts.shape
    return parts.reshape(*lengths[:dim], lengths[dim] * lengths[dim + 1], *lengths[dim + 2 :])


def sent_to_all(value, axis):
    devices = lax.axis_size(axis)
    return lax.all_to_all(
        jnp.broadcast_to(value[None], (devices, *value.shape)), axis, 0, 0, tiled=True
    )


def collect(value, axis, dim):
    return laid_out(sent_to_all(value, axis), dim)


def leaf_block(source, remote, values, active):
    distance = source[:, None, :, :, None] - remote[:, :, :, None, :]
    kernel = (
        active[:, :, None, None] / jnp.sqrt(jnp.sum(distance * distance, axis=2) + softening)
    ).astype(jnp.bfloat16)
    return jnp.einsum("lsij,lsrj->lri", kernel, values, preferred_element_type=jnp.float32)


def to_grid(flat, depth, upper, per_leaf):
    shaped = flat.reshape(depth, upper, 2, 2, 2, 2, 2, 2, per_leaf)
    moved = shaped.transpose(4, 7, 3, 6, 1, 2, 5, 0, 8)
    return moved.reshape(BX, BY, upper * 4, depth * per_leaf)


def shards(
    charges,
    points,
    leaf_basis,
    transfer_one,
    transfer_two,
    couple_one,
    couple_two,
    near_list,
    list_one,
    list_two,
):
    rhs_count, columns = charges.shape
    leaves = near_list.shape[0]
    per_leaf = columns // leaves
    rank_size = leaf_basis.shape[0]
    col_size = lax.axis_size("col")
    upper = leaves // 64
    depth_z = upper * 4
    charge_grid = to_grid(charges, rhs_count, upper, per_leaf)
    point_grid = to_grid(points, 3, upper, per_leaf)
    mask_grid = (
        near_list.reshape(upper, 2, 2, 2, 2, 2, 2, 27)
        .transpose(3, 6, 2, 5, 0, 1, 4, 7)
        .reshape(BX, BY, depth_z, 27)
    )
    wide_charges = padded(charge_grid, (("row", 1), ("col", 0)), 1)
    wide_points = padded(point_grid, (("row", 1), ("col", 0)), 1)
    wide_charges = jnp.pad(wide_charges, ((0, 0), (0, 0), (1, 1), (0, 0)))
    wide_points = jnp.pad(wide_points, ((0, 0), (0, 0), (1, 1), (0, 0)))
    block_leaves = BX * BY

    def near_step(layer_index):
        charge_layer = lax.dynamic_slice_in_dim(wide_charges, layer_index, 3, 2)
        point_layer = lax.dynamic_slice_in_dim(wide_points, layer_index, 3, 2)
        own_points = lax.dynamic_slice_in_dim(point_grid, layer_index, 1, 2)
        own_mask = lax.dynamic_slice_in_dim(mask_grid, layer_index, 1, 2)
        value_list = []
        place_list = []
        for step_z in range(3):
            for step_y in range(3):
                for step_x in range(3):
                    value_list.append(
                        charge_layer[step_x : step_x + BX, step_y : step_y + BY, step_z]
                    )
                    place_list.append(
                        point_layer[step_x : step_x + BX, step_y : step_y + BY, step_z]
                    )
        values = jnp.stack(value_list, axis=2).reshape(block_leaves, 27, rhs_count, per_leaf)
        remote = jnp.stack(place_list, axis=2).reshape(block_leaves, 27, 3, per_leaf)
        source = own_points.reshape(block_leaves, 3, per_leaf)
        active = (own_mask.reshape(block_leaves, 27) >= 0).astype(jnp.float32)
        return leaf_block(source, remote, values, active)

    near_layers = lax.map(near_step, jnp.arange(depth_z, dtype=jnp.int32))
    near_part = (
        near_layers.reshape(upper, 2, 2, 2, 2, 2, 2, rhs_count, per_leaf)
        .transpose(7, 0, 1, 5, 3, 2, 6, 4, 8)
        .reshape(rhs_count, leaves, per_leaf)
    )
    charge_leaf = charges.reshape(rhs_count, leaves, per_leaf)
    basis_leaf = leaf_basis.reshape(rank_size, leaves, per_leaf)
    coef_leaf = jnp.einsum(
        "kln,rln->lkr", basis_leaf, charge_leaf, preferred_element_type=jnp.float32
    ).astype(jnp.bfloat16)
    nodes_one = leaves // 8
    lifted = jnp.einsum("lab,lar->lbr", transfer_one, coef_leaf, preferred_element_type=jnp.float32)
    coef_one = lifted.reshape(nodes_one, 8, rank_size, rhs_count).sum(axis=1).astype(jnp.bfloat16)
    lifted_two = jnp.einsum(
        "lab,lar->lbr", transfer_two, coef_one, preferred_element_type=jnp.float32
    )
    coef_two = (
        lifted_two.reshape(nodes_one // 8, 8, rank_size, rhs_count).sum(axis=1).astype(jnp.bfloat16)
    )
    gathered, group_top = (collect(coef_one, "col", 0), collect(coef_two, "col", 0))
    every_top = collect(group_top, "row", 0)
    group_start = lax.axis_index("row") * col_size * nodes_one
    partner_ids = jnp.clip(list_one - group_start, 0, col_size * nodes_one - 1)
    active = (list_one >= 0).astype(jnp.bfloat16)
    partner = gathered[partner_ids] * active[:, :, None, None]
    field_one = jnp.einsum(
        "psab,psbr->par", couple_one, partner, preferred_element_type=jnp.float32
    )
    field_two = jnp.einsum(
        "psab,psbr->par", couple_two, every_top[list_two], preferred_element_type=jnp.float32
    )
    down_one = field_one + jnp.einsum(
        "pab,pbr->par",
        transfer_two.astype(jnp.float32),
        jnp.repeat(field_two, 8, axis=0),
        precision=lax.Precision.HIGHEST,
    )
    down_leaf = jnp.einsum(
        "lab,lbr->lar",
        transfer_one.astype(jnp.float32),
        jnp.repeat(down_one, 8, axis=0),
        precision=lax.Precision.HIGHEST,
    ).astype(jnp.bfloat16)
    far_part = jnp.einsum("kln,lkr->rln", basis_leaf, down_leaf, preferred_element_type=jnp.float32)
    potential = near_part * (NEAR * PTS) ** (-0.5) + far_part
    return potential.reshape(rhs_count, leaves * per_leaf).astype(jnp.bfloat16)


def solution(mesh):
    in_specs = (
        P(None, ("row", "col")),
        P(None, ("row", "col")),
        P(None, ("row", "col")),
        P(("row", "col"), None, None),
        P(("row", "col"), None, None),
        P(("row", "col"), None, None, None),
        P(("row", "col"), None, None, None),
        P(("row", "col"), None),
        P(("row", "col"), None),
        P(("row", "col"), None),
    )
    out_specs = P(None, ("row", "col"))
    return jax.shard_map(shards, mesh=mesh, in_specs=in_specs, out_specs=out_specs, check_vma=False)
```

profile of v0, /device:TPU:1, one launch (start us, length us, event | category | flops | bytes accessed | tf_op | source)
XLA Modules:
  0.0 436.6 jit_solution(2434485273149556583)
XLA Ops:
  0.0 3.6 reshape.87
  3.6 1.9 copy.159
  6.2 1.3 fusion.32
  7.5 4.7 %collective-permute-start = (bf16[4,1,4,4096]{3,1,0,2:T(2,128)(2,1)}, bf16[4,1,4,4096]{3,1,0,2:T(2,128)(2,1)S(1)}, u32[]{:S(2)}, u32[]{:S(2)}) collective-permute-start(bf16[4,1,4,4096]{3,1,0,2:T(2,128)(2,1)} %get-tuple-element.115), channel_id=1, source_target_pairs={{0,8},{8,16},{16,24},{24,32},{32,40},{40,48},{48,56},{56,64},{64,7... | collective-permute-start | bytes 393224 | tf_op jit(solution)/shard_map/ppermute | solution.py:22
  12.3 1.9 collective-permute-start.1
  14.6 3.6 collective-permute-start.4
  18.2 1.9 collective-permute-start.5
  20.1 2.1 reshape.94
  22.2 1.7 copy.77
  24.0 1.7 reshape.93
  25.6 2.8 bitcast_reduce_fusion
  29.4 6.4 %all-to-all-start.1 = ((bf16[8,2,1024]{2,1,0:T(2,128)(2,1)}), bf16[8,2,1024]{2,1,0:T(2,128)(2,1)S(1)}, u32[]{:S(2)}, u32[]{:S(2)}) async-start(bf16[8,2,1024]{2,1,0:T(2,128)(2,1)} %reshape.131), calls=%async_computation.1 | async-start | bytes 65536 | tf_op jit(solution)/shard_map/all_to_all | solution.py:36
  37.1 4.9 %collective-permute-start.6 = (f32[1,6,4,192]{3,2,1,0:T(4,128)S(1)}, f32[1,6,4,192]{3,2,1,0:T(4,128)S(1)}, u32[]{:S(2)}, u32[]{:S(2)}) collective-permute-start(f32[1,6,4,192]{3,2,1,0:T(4,128)S(1)} %get-tuple-element.117), channel_id=1, source_target_pairs={{0,1},{1,2},{2,3},{3,4},{4,5},{5,6},{6,7},{8,9},{9,10},{10,11},{11... | collective-permute-start | bytes 55304 | tf_op jit(solution)/shard_map/ppermute | solution.py:22
  42.0 1.3 collective-permute-start.7
  44.7 1.1 reshape.129
  45.8 7.3 %all-to-all-start = ((bf16[8,2,8192]{2,1,0:T(2,128)(2,1)}), bf16[8,2,8192]{2,1,0:T(2,128)(2,1)S(1)}, u32[]{:S(2)}, u32[]{:S(2)}) async-start(bf16[8,2,8192]{2,1,0:T(2,128)(2,1)} %reshape.129), calls=%async_computation | async-start | bytes 524288 | tf_op jit(solution)/shard_map/all_to_all | solution.py:36
  53.2 1.8 broadcast_in_dim.43
  55.0 4.6 %reshape.133 = bf16[32,2,8192]{2,1,0:T(2,128)(2,1)} reshape(bf16[32,8,32,64]{3,2,1,0:T(8,128)(2,1)} %broadcast_in_dim.43) | data formatting | bytes 2097152
  59.7 1.4 pad_maximum_fusion.2
  61.1 4.9 %collective-permute-start.2 = (bf16[1,6,4,4096]{3,1,0,2:T(8,128)(2,1)S(1)}, bf16[1,6,4,4096]{3,1,0,2:T(8,128)(2,1)S(1)}, u32[]{:S(2)}, u32[]{:S(2)}) collective-permute-start(bf16[1,6,4,4096]{3,1,0,2:T(8,128)(2,1)S(1)} %get-tuple-element.113), channel_id=1, source_target_pairs={{0,1},{1,2},{2,3},{3,4},{4,5},{5,6},{6,7},{8,9},{9,10},{10,11},{11... | collective-permute-start | bytes 589832 | tf_op jit(solution)/shard_map/ppermute | solution.py:22
  66.0 1.3 collective-permute-start.3
  67.3 15.7 %all-to-all-start.2 = ((bf16[32,2,8192]{2,1,0:T(2,128)(2,1)}), bf16[32,2,8192]{2,1,0:T(2,128)(2,1)}, u32[]{:S(2)}, u32[]{:S(2)}) async-start(bf16[32,2,8192]{2,1,0:T(2,128)(2,1)} %reshape.133), calls=%async_computation.2 | async-start | bytes 2097152 | tf_op jit(solution)/shard_map/all_to_all | solution.py:36
  83.4 0.8 gather_fusion
  84.3 1.8 convolution_bitcast_fusion
  86.8 2.2 select_maximum_fusion
  89.0 332.4 %while.10 = (s32[]{:T(128)}, f32[4,16,64,64]{3,2,1,0:T(8,128)}, s32[4]{0:T(128)S(1)}, bf16[6,6,6,4096]{3,1,0,2:T(8,128)(2,1)S(1)}, s32[4,4,4,27]{3,2,1,0:T(4,128...) while((s32[]{:T(128)}, f32[4,16,64,64]{3,2,1,0:T(8,128)}, ...), condition=%wide.region_2.3_spmd, body=%wide.region_0.2_spmd.sunk | while | flops 245957488 | bytes 45520492 | solution.py:113
  110.8 10.9 %reshape.136 = bf16[16,27,64,64]{3,2,0,1:T(8,128)(2,1)} reshape(bf16[4,4,27,4096]{3,1,0,2:T(4,128)(2,1)} %dynamic-slice_dynamic-update-slice_fusion.80) | data formatting | bytes 7077888 | tf_op jit(solution)/shard_map/while/body/eval_jaxpr/reshape | solution.py:107
  140.1 2.3 sub.39
  142.5 18.7 %multiply_reduce_fusion.2 = f32[16,27,64,64]{3,2,1,0:T(8,128)} fusion(f32[16,3,64]{2,1,0:T(4,128)S(1)} %sub.38, f32[16,27,3,64]{3,2,0,1:T(4,128)} %sub.39), kind=kLoop, calls=%fused_computation.2.clone.1 | loop fusion | flops 14155776 | bytes 7421952 | tf_op jit(solution)/shard_map/while/body/eval_jaxpr/reduce_sum | solution.py:48
  162.0 10.2 %fusion.53 = f32[4,16,64,64]{3,2,1,0:T(8,128)} fusion(f32[4,16,64,64]{3,2,1,0:T(8,128)} %get-tuple-element.234, s32[]{:T(128)} %get-tuple-element.233, bf16[16,27,64,64]{3,2,0,1:T(8,128)(2,1)} %reshape.136, f32[16,27,64,64]{3,2,1,0:T(8,128)} %multiply_reduce_fusion.2, f32[16,27]{1,0:T(8,128)S(1)} %bitcast.99), kind=kOutput, calls=%fused_computation.7.clone.1 | convolution fusion | flops 231800832 | bytes 21760192 | tf_op jit(solution)/shard_map/while/body/eval_jaxpr/lsij,lsrj->lri/dot_general | solution.py:50
  193.9 10.9 %reshape.136 = bf16[16,27,64,64]{3,2,0,1:T(8,128)(2,1)} reshape(bf16[4,4,27,4096]{3,1,0,2:T(4,128)(2,1)} %dynamic-slice_dynamic-update-slice_fusion.80) | data formatting | bytes 7077888 | tf_op jit(solution)/shard_map/while/body/eval_jaxpr/reshape | solution.py:107
  223.1 2.3 sub.39
  225.6 18.7 %multiply_reduce_fusion.2 = f32[16,27,64,64]{3,2,1,0:T(8,128)} fusion(f32[16,3,64]{2,1,0:T(4,128)S(1)} %sub.38, f32[16,27,3,64]{3,2,0,1:T(4,128)} %sub.39), kind=kLoop, calls=%fused_computation.2.clone.1 | loop fusion | flops 14155776 | bytes 7421952 | tf_op jit(solution)/shard_map/while/body/eval_jaxpr/reduce_sum | solution.py:48
  245.0 10.2 %fusion.53 = f32[4,16,64,64]{3,2,1,0:T(8,128)} fusion(f32[4,16,64,64]{3,2,1,0:T(8,128)} %get-tuple-element.234, s32[]{:T(128)} %get-tuple-element.233, bf16[16,27,64,64]{3,2,0,1:T(8,128)(2,1)} %reshape.136, f32[16,27,64,64]{3,2,1,0:T(8,128)} %multiply_reduce_fusion.2, f32[16,27]{1,0:T(8,128)S(1)} %bitcast.99), kind=kOutput, calls=%fused_computation.7.clone.1 | convolution fusion | flops 231800832 | bytes 21760192 | tf_op jit(solution)/shard_map/while/body/eval_jaxpr/lsij,lsrj->lri/dot_general | solution.py:50
  277.0 10.9 %reshape.136 = bf16[16,27,64,64]{3,2,0,1:T(8,128)(2,1)} reshape(bf16[4,4,27,4096]{3,1,0,2:T(4,128)(2,1)} %dynamic-slice_dynamic-update-slice_fusion.80) | data formatting | bytes 7077888 | tf_op jit(solution)/shard_map/while/body/eval_jaxpr/reshape | solution.py:107
  306.2 2.3 sub.39
  308.7 18.7 %multiply_reduce_fusion.2 = f32[16,27,64,64]{3,2,1,0:T(8,128)} fusion(f32[16,3,64]{2,1,0:T(4,128)S(1)} %sub.38, f32[16,27,3,64]{3,2,0,1:T(4,128)} %sub.39), kind=kLoop, calls=%fused_computation.2.clone.1 | loop fusion | flops 14155776 | bytes 7421952 | tf_op jit(solution)/shard_map/while/body/eval_jaxpr/reduce_sum | solution.py:48
  328.1 10.2 %fusion.53 = f32[4,16,64,64]{3,2,1,0:T(8,128)} fusion(f32[4,16,64,64]{3,2,1,0:T(8,128)} %get-tuple-element.234, s32[]{:T(128)} %get-tuple-element.233, bf16[16,27,64,64]{3,2,0,1:T(8,128)(2,1)} %reshape.136, f32[16,27,64,64]{3,2,1,0:T(8,128)} %multiply_reduce_fusion.2, f32[16,27]{1,0:T(8,128)S(1)} %bitcast.99), kind=kOutput, calls=%fused_computation.7.clone.1 | convolution fusion | flops 231800832 | bytes 21760192 | tf_op jit(solution)/shard_map/while/body/eval_jaxpr/lsij,lsrj->lri/dot_general | solution.py:50
  360.1 10.9 %reshape.136 = bf16[16,27,64,64]{3,2,0,1:T(8,128)(2,1)} reshape(bf16[4,4,27,4096]{3,1,0,2:T(4,128)(2,1)} %dynamic-slice_dynamic-update-slice_fusion.80) | data formatting | bytes 7077888 | tf_op jit(solution)/shard_map/while/body/eval_jaxpr/reshape | solution.py:107
  389.3 2.3 sub.39
  391.7 18.7 %multiply_reduce_fusion.2 = f32[16,27,64,64]{3,2,1,0:T(8,128)} fusion(f32[16,3,64]{2,1,0:T(4,128)S(1)} %sub.38, f32[16,27,3,64]{3,2,0,1:T(4,128)} %sub.39), kind=kLoop, calls=%fused_computation.2.clone.1 | loop fusion | flops 14155776 | bytes 7421952 | tf_op jit(solution)/shard_map/while/body/eval_jaxpr/reduce_sum | solution.py:48
  411.2 10.2 %fusion.53 = f32[4,16,64,64]{3,2,1,0:T(8,128)} fusion(f32[4,16,64,64]{3,2,1,0:T(8,128)} %get-tuple-element.234, s32[]{:T(128)} %get-tuple-element.233, bf16[16,27,64,64]{3,2,0,1:T(8,128)(2,1)} %reshape.136, f32[16,27,64,64]{3,2,1,0:T(8,128)} %multiply_reduce_fusion.2, f32[16,27]{1,0:T(8,128)S(1)} %bitcast.99), kind=kOutput, calls=%fused_computation.7.clone.1 | convolution fusion | flops 231800832 | bytes 21760192 | tf_op jit(solution)/shard_map/while/body/eval_jaxpr/lsij,lsrj->lri/dot_general | solution.py:50
  421.4 1.8 broadcast_multiply_fusion
  423.4 4.7 %reshape.134 = bf16[32,8,32,64]{3,2,1,0:T(8,128)(2,1)} reshape(bf16[32,2,8192]{2,1,0:T(2,128)(2,1)} %all-to-all-done.2) | data formatting | bytes 2097152
  428.1 2.3 gather_fusion.1
  430.9 1.7 convolution_convert_fusion
  432.6 1.7 fusion.14
  435.0 1.6 convert_element_type.59
  (328 shorter events, 158.0 us)
Async XLA Ops:
  0.0 84.3 %copy-start = (bf16[8,12,32,32]{3,2,1,0:T(8,128)(2,1)S(1)}, bf16[8,12,32,32]{3,2,1,0:T(8,128)(2,1)}, u32[]{:S(2)}) copy-start(bf16[8,12,32,32]{3,2,1,0:T(8,128)(2,1)} %param.17) | copy-start | bytes 589828
  0.0 20.1 %copy-start.2 = (bf16[64,4096]{1,0:T(8,128)(2,1)S(1)}, bf16[64,4096]{1,0:T(8,128)(2,1)}, u32[]{:S(2)}) copy-start(bf16[64,4096]{1,0:T(8,128)(2,1)} %param.12) | copy-start | bytes 1572868
  0.0 14.2 %copy-start.11 = (f32[3,4096]{1,0:T(4,128)S(1)}, f32[3,4096]{1,0:T(4,128)}, u32[]{:S(2)}) copy-start(f32[3,4096]{1,0:T(4,128)} %param.13) | copy-start | bytes 147460
  6.2 53.6 %copy-start.1 = (bf16[4,4,4,4096]{3,1,0,2:T(4,128)(2,1)}, bf16[4,4,4,4096]{3,1,0,2:T(4,128)(2,1)S(1)}, u32[]{:S(2)}) copy-start(bf16[4,4,4,4096]{3,1,0,2:T(4,128)(2,1)S(1)} %reshape.88) | copy-start | bytes 1572868
  6.2 22.3 %copy-start.6 = (bf16[8,32,32]{2,1,0:T(8,128)(2,1)S(1)}, bf16[8,32,32]{2,1,0:T(8,128)(2,1)}, u32[]{:S(2)}) copy-start(bf16[8,32,32]{2,1,0:T(8,128)(2,1)} %param.16) | copy-start | bytes 49156
  7.5 28.2 %copy-start.14 = (s32[1,16]{1,0:T(1,128)S(1)}, s32[1,16]{1,0:T(1,128)}, u32[]{:S(2)}) copy-start(s32[1,16]{1,0:T(1,128)} %param.21) | copy-start | bytes 196
  7.5 28.2 %copy-start.13 = (s32[8,12]{1,0:T(8,128)S(1)}, s32[8,12]{1,0:T(8,128)}, u32[]{:S(2)}) copy-start(s32[8,12]{1,0:T(8,128)} %param.20) | copy-start | bytes 1156
  7.5 36.3 %copy-start.12 = (s32[64,27]{0,1:T(8,128)S(1)}, s32[64,27]{0,1:T(8,128)}, u32[]{:S(2)}) copy-start(s32[64,27]{0,1:T(8,128)} %param.19) | copy-start | bytes 20740
  7.5 52.2 %collective-permute-start = (bf16[4,1,4,4096]{3,1,0,2:T(2,128)(2,1)}, bf16[4,1,4,4096]{3,1,0,2:T(2,128)(2,1)S(1)}, u32[]{:S(2)}, u32[]{:S(2)}) collective-permute-start(bf16[4,1,4,4096]{3,1,0,2:T(2,128)(2,1)} %get-tuple-element.115), channel_id=1, source_target_pairs={{0,8},{8,16},{16,24},{24,32},{32,40},{40,48},{48,56},{56,64},{64,7... | collective-permute-start | bytes 393224 | tf_op jit(solution)/shard_map/ppermute | solution.py:22
  12.3 47.5 %collective-permute-start.1 = (bf16[4,1,4,4096]{3,1,0,2:T(2,128)(2,1)}, bf16[4,1,4,4096]{3,1,0,2:T(2,128)(2,1)}, u32[]{:S(2)}, u32[]{:S(2)}) collective-permute-start(bf16[4,1,4,4096]{3,1,0,2:T(2,128)(2,1)} %get-tuple-element.116), channel_id=1, source_target_pairs={{8,0},{16,8},{24,16},{32,24},{40,32},{48,40},{56,48},{64,56},{72,6... | collective-permute-start | bytes 393224 | tf_op jit(solution)/shard_map/ppermute | solution.py:23
  14.6 22.5 %collective-permute-start.4 = (f32[4,1,4,192]{3,2,1,0:T(4,128)S(1)}, f32[4,1,4,192]{3,2,1,0:T(4,128)S(1)}, u32[]{:S(2)}, u32[]{:S(2)}) collective-permute-start(f32[4,1,4,192]{3,2,1,0:T(4,128)S(1)} %get-tuple-element.120), channel_id=1, source_target_pairs={{0,8},{8,16},{16,24},{24,32},{32,40},{40,48},{48,56},{56,64},{64,7... | collective-permute-start | bytes 36872 | tf_op jit(solution)/shard_map/ppermute | solution.py:22
  18.2 18.9 %collective-permute-start.5 = (f32[4,1,4,192]{3,2,1,0:T(4,128)S(1)}, f32[4,1,4,192]{3,2,1,0:T(4,128)S(1)}, u32[]{:S(2)}, u32[]{:S(2)}) collective-permute-start(f32[4,1,4,192]{3,2,1,0:T(4,128)S(1)} %get-tuple-element.119), channel_id=1, source_target_pairs={{8,0},{16,8},{24,16},{32,24},{40,32},{48,40},{56,48},{64,56},{72,6... | collective-permute-start | bytes 36872 | tf_op jit(solution)/shard_map/ppermute | solution.py:23
  24.0 20.6 %copy-start.3 = (bf16[64,32,32]{2,1,0:T(8,128)(2,1)}, bf16[64,32,32]{2,1,0:T(8,128)(2,1)S(1)}, u32[]{:S(2)}) copy-start(bf16[64,32,32]{2,1,0:T(8,128)(2,1)S(1)} %copy.77) | copy-start | bytes 393220
  25.6 29.4 %copy-start.4 = (bf16[32,64,64]{2,1,0:T(8,128)(2,1)}, bf16[32,64,64]{2,1,0:T(8,128)(2,1)S(1)}, u32[]{:S(2)}) copy-start(bf16[32,64,64]{2,1,0:T(8,128)(2,1)S(1)} %reshape.93) | copy-start | bytes 786436
  29.4 16.4 %all-to-all-start.1 = ((bf16[8,2,1024]{2,1,0:T(2,128)(2,1)}), bf16[8,2,1024]{2,1,0:T(2,128)(2,1)S(1)}, u32[]{:S(2)}, u32[]{:S(2)}) async-start(bf16[8,2,1024]{2,1,0:T(2,128)(2,1)} %reshape.131), calls=%async_computation.1 | async-start | bytes 65536 | tf_op jit(solution)/shard_map/all_to_all | solution.py:36
  37.1 22.5 %collective-permute-start.6 = (f32[1,6,4,192]{3,2,1,0:T(4,128)S(1)}, f32[1,6,4,192]{3,2,1,0:T(4,128)S(1)}, u32[]{:S(2)}, u32[]{:S(2)}) collective-permute-start(f32[1,6,4,192]{3,2,1,0:T(4,128)S(1)} %get-tuple-element.117), channel_id=1, source_target_pairs={{0,1},{1,2},{2,3},{3,4},{4,5},{5,6},{6,7},{8,9},{9,10},{10,11},{11... | collective-permute-start | bytes 55304 | tf_op jit(solution)/shard_map/ppermute | solution.py:22
  42.0 17.7 %collective-permute-start.7 = (f32[1,6,4,192]{3,2,1,0:T(4,128)S(1)}, f32[1,6,4,192]{3,2,1,0:T(4,128)S(1)}, u32[]{:S(2)}, u32[]{:S(2)}) collective-permute-start(f32[1,6,4,192]{3,2,1,0:T(4,128)S(1)} %get-tuple-element.118), channel_id=1, source_target_pairs={{1,0},{2,1},{3,2},{4,3},{5,4},{6,5},{7,6},{9,8},{10,9},{11,10},{12... | collective-permute-start | bytes 55304 | tf_op jit(solution)/shard_map/ppermute | solution.py:23
  45.8 21.5 %all-to-all-start = ((bf16[8,2,8192]{2,1,0:T(2,128)(2,1)}), bf16[8,2,8192]{2,1,0:T(2,128)(2,1)S(1)}, u32[]{:S(2)}, u32[]{:S(2)}) async-start(bf16[8,2,8192]{2,1,0:T(2,128)(2,1)} %reshape.129), calls=%async_computation | async-start | bytes 524288 | tf_op jit(solution)/shard_map/all_to_all | solution.py:36
  59.7 26.4 %copy-start.5 = (bf16[4,1,4,4096]{3,1,0,2:T(2,128)(2,1)}, bf16[4,1,4,4096]{3,1,0,2:T(2,128)(2,1)S(1)}, u32[]{:S(2)}) copy-start(bf16[4,1,4,4096]{3,1,0,2:T(2,128)(2,1)S(1)} %collective-permute-done) | copy-start | bytes 393220
  61.1 24.9 %collective-permute-start.2 = (bf16[1,6,4,4096]{3,1,0,2:T(8,128)(2,1)S(1)}, bf16[1,6,4,4096]{3,1,0,2:T(8,128)(2,1)S(1)}, u32[]{:S(2)}, u32[]{:S(2)}) collective-permute-start(bf16[1,6,4,4096]{3,1,0,2:T(8,128)(2,1)S(1)} %get-tuple-element.113), channel_id=1, source_target_pairs={{0,1},{1,2},{2,3},{3,4},{4,5},{5,6},{6,7},{8,9},{9,10},{10,11},{11... | collective-permute-start | bytes 589832 | tf_op jit(solution)/shard_map/ppermute | solution.py:22
  66.0 20.8 %collective-permute-start.3 = (bf16[1,6,4,4096]{3,1,0,2:T(8,128)(2,1)S(1)}, bf16[1,6,4,4096]{3,1,0,2:T(8,128)(2,1)}, u32[]{:S(2)}, u32[]{:S(2)}) collective-permute-start(bf16[1,6,4,4096]{3,1,0,2:T(8,128)(2,1)S(1)} %get-tuple-element.114), channel_id=1, source_target_pairs={{1,0},{2,1},{3,2},{4,3},{5,4},{6,5},{7,6},{9,8},{10,9},{11,10},{12... | collective-permute-start | bytes 589832 | tf_op jit(solution)/shard_map/ppermute | solution.py:23
  67.3 356.0 %all-to-all-start.2 = ((bf16[32,2,8192]{2,1,0:T(2,128)(2,1)}), bf16[32,2,8192]{2,1,0:T(2,128)(2,1)}, u32[]{:S(2)}, u32[]{:S(2)}) async-start(bf16[32,2,8192]{2,1,0:T(2,128)(2,1)} %reshape.133), calls=%async_computation.2 | async-start | bytes 2097152 | tf_op jit(solution)/shard_map/all_to_all | solution.py:36
  86.1 0.7 copy-start.8
  89.0 21.8 %copy-start.15 = (s32[4]{0:T(128)}, s32[4]{0:T(128)S(1)}, u32[]{:S(2)}) copy-start(s32[4]{0:T(128)S(1)} %get-tuple-element.248) | copy-start | bytes 52 | tf_op jit(solution)/shard_map/while
  161.9 10.2 %copy-start.16 = (s32[4]{0:T(128)S(1)}, s32[4]{0:T(128)}, u32[]{:S(2)}) copy-start(s32[4]{0:T(128)} %copy-done.15) | copy-start | bytes 52 | tf_op jit(solution)/shard_map/while
  172.1 21.8 %copy-start.15 = (s32[4]{0:T(128)}, s32[4]{0:T(128)S(1)}, u32[]{:S(2)}) copy-start(s32[4]{0:T(128)S(1)} %get-tuple-element.248) | copy-start | bytes 52 | tf_op jit(solution)/shard_map/while
  245.0 10.2 %copy-start.16 = (s32[4]{0:T(128)S(1)}, s32[4]{0:T(128)}, u32[]{:S(2)}) copy-start(s32[4]{0:T(128)} %copy-done.15) | copy-start | bytes 52 | tf_op jit(solution)/shard_map/while
  255.2 21.8 %copy-start.15 = (s32[4]{0:T(128)}, s32[4]{0:T(128)S(1)}, u32[]{:S(2)}) copy-start(s32[4]{0:T(128)S(1)} %get-tuple-element.248) | copy-start | bytes 52 | tf_op jit(solution)/shard_map/while
  328.1 10.2 %copy-start.16 = (s32[4]{0:T(128)S(1)}, s32[4]{0:T(128)}, u32[]{:S(2)}) copy-start(s32[4]{0:T(128)} %copy-done.15) | copy-start | bytes 52 | tf_op jit(solution)/shard_map/while
  338.3 21.8 %copy-start.15 = (s32[4]{0:T(128)}, s32[4]{0:T(128)S(1)}, u32[]{:S(2)}) copy-start(s32[4]{0:T(128)S(1)} %get-tuple-element.248) | copy-start | bytes 52 | tf_op jit(solution)/shard_map/while
  411.2 10.2 %copy-start.16 = (s32[4]{0:T(128)S(1)}, s32[4]{0:T(128)}, u32[]{:S(2)}) copy-start(s32[4]{0:T(128)} %copy-done.15) | copy-start | bytes 52 | tf_op jit(solution)/shard_map/while
  423.2 7.2 %copy-start.9 = (bf16[1,16,32,32]{3,2,1,0:T(8,128)(2,1)S(1)}, bf16[1,16,32,32]{3,2,1,0:T(8,128)(2,1)}, u32[]{:S(2)}) copy-start(bf16[1,16,32,32]{3,2,1,0:T(8,128)(2,1)} %param.18) | copy-start | bytes 98308
  423.2 7.4 %copy-start.7 = (bf16[8,32,32]{2,1,0:T(8,128)(2,1)S(1)}, bf16[8,32,32]{2,1,0:T(8,128)(2,1)}, u32[]{:S(2)}) copy-start(bf16[8,32,32]{2,1,0:T(8,128)(2,1)} %param.16) | copy-start | bytes 49156
  423.2 7.4 %copy-start.10 = (f32[8,64,32]{1,2,0:T(8,128)S(1)}, f32[8,64,32]{1,2,0:T(8,128)}, u32[]{:S(2)}) copy-start(f32[8,64,32]{1,2,0:T(8,128)} %convolution_bitcast_fusion) | copy-start | bytes 196612
where the time goes:
time: 441 us; the launch traced here: 437 us
  local copies, waits for them, and re-layouts  238 us (54%)
  other arithmetic  82 us (19%)
  starting transfers between devices  53.9 us (12%)
  matrix products  49.2 us (11%)
  loops' own time  13.2 us (3%)
    while x224, local copies, waits for them, and re-layouts  137 us
    reduce_sum x4, other arithmetic, leaf_block(): jnp.sum(distance * distance, axis=2) + softening  74.7 us
    reshape x4, local copies, waits for them, and re-layouts, near_step(): jnp.stack(value_list, axis=2).reshape(block_leaves, 27, rhs_count, per_leaf)  43.7 us
    dot_general x4, matrix products, leaf_block(): jnp.einsum('lsij,lsrj->lri', kernel, values, preferred_element_type=jnp.f...  40.7 us
    all_to_all x3, starting transfers between devices, sent_to_all(): lax.all_to_all(jnp.broadcast_to(value[None], (devices, *value.shape)), ax...  29.3 us
    ppermute x4, starting transfers between devices, padded(): before = lax.ppermute(last, axis, up)  18.1 us
    unnamed x40, local copies, waits for them, and re-layouts  14.2 us
    another operation x1, loops' own time, shards(): near_layers = lax.map(near_step, jnp.arange(depth_z, dtype=jnp.int32))  13.2 us
  transfers between devices with their start and end apart: 11, of which 0 were waited for; matrix products, arithmetic and copies ran while one was open for 80% of the time, Pallas kernels for 0%

commit v1 on v0

v1 whole, which is shorter than its diff:
```python
import jax
import jax.numpy as jnp
import numpy as np
from jax import lax
from jax.experimental import pallas as pl
from jax.experimental.pallas import tpu as pltpu
from jax.sharding import PartitionSpec as P

F32 = jnp.float32
BF16 = jnp.bfloat16
MESH = pl.DeviceIdType.MESH
NT = (((1,), (1,)), ((), ()))
TN = (((0,), (0,)), ((), ()))
NN = (((1,), (0,)), ((), ()))

ROWS = 32
COLS = 8
SOFT = 0.0025
SCALE = (27 * 64) ** (-0.5)


def mm(a, b, dims=NN):
    return lax.dot_general(a, b, dims, preferred_element_type=F32)


def picks():
    pick = np.zeros((256, 192), np.float32)
    sides = (((0, 1, 1, 2, 3), (0, -1, 1, 0, -1)), ((0, 1, 2, 2, 3), (1, 0, -1, 1, 0)))
    for side, (places, steps) in enumerate(sides):
        for x in range(4):
            for y in range(4):
                for tile in range(5):
                    z = places[tile]
                    leaf = x % 2 + 2 * (y % 2) + 4 * (z % 2) + 8 * (x // 2) + 16 * (y // 2) + 32 * (z // 2)
                    pick[side * 128 + (x * 4 + y) * 8 + tile, (steps[tile] + 1) * 64 + leaf] = 1
    return pick


def body(
    charges,
    points,
    basis,
    t_one,
    t_two,
    c_one,
    c_two,
    near_list,
    list_one,
    list_two,
    pick,
    out,
    ext_c,
    ext_p,
    wide_c,
    src_f,
    own_f,
    masks,
    shifted,
    near,
    split_basis,
    coef,
    one_send,
    one_all,
    two_send,
    two_all,
    ctwo_send,
    ctwo_all,
    lists_send,
    lists_all,
    lists_s,
    chosen,
    field,
    part_send,
    part_all,
    halo_s,
    halo_r,
    one_s,
    one_r,
    two_s,
    two_r,
    ctwo_s,
    ctwo_r,
    lt_s,
    lt_r,
    part_s,
    part_r,
    local,
):
    r = lax.axis_index("row")
    c = lax.axis_index("col")
    barrier = pltpu.get_barrier_semaphore()

    def greet_col(k, _):
        pl.semaphore_signal(barrier, inc=1, device_id=(r, lax.rem(c + k, COLS)), device_id_type=MESH)
        return 0

    def greet_row(k, _):
        pl.semaphore_signal(barrier, inc=1, device_id=(lax.rem(r + k, ROWS), c), device_id_type=MESH)
        return 0

    lax.fori_loop(1, COLS, greet_col, 0)
    lax.fori_loop(1, ROWS, greet_row, 0)

    low = lax.broadcasted_iota(jnp.int32, (64, 128), 1) < 64

    def halves(a, b, upper):
        if upper:
            return jnp.concatenate([a[:, 64:], b[:, 64:]], axis=1)
        return jnp.concatenate([a[:, :64], b[:, :64]], axis=1)

    def arrange(i, _):
        x1, y = i // 4, lax.rem(i, 4)
        for h in range(2):
            tile = lax.rem(y, 2) + 4 * x1 + 8 * (y // 2) + 16 * h
            first = pl.ds(pl.multiple_of(tile * 128, 128), 128)
            second = pl.ds(pl.multiple_of(tile * 128 + 256, 128), 128)
            at = slice(h * 128, h * 128 + 128)
            a, b = charges[:, first], charges[:, second]
            pa, pb = points[:, first], points[:, second]
            for x0 in range(2):
                ext_c[1 + y, 1 + 2 * x1 + x0, :, at] = halves(a, b, x0)
                ext_p[1 + y, 1 + 2 * x1 + x0, 0:3, at] = halves(pa, pb, x0)
                ext_p[1 + y, 1 + 2 * x1 + x0, 3:4, at] = jnp.zeros((1, 128), F32)
        return 0

    lax.fori_loop(0, 8, arrange, 0)

    ctwo_send[...] = jnp.concatenate([c_two[s] for s in range(16)], axis=1)
    lists_send[...] = jnp.zeros_like(lists_send)
    lists_send[0:1, 0:16] = list_two[...]

    pl.semaphore_wait(barrier, COLS + ROWS - 2)

    def halo(n, ref, src, dst, device):
        return pltpu.make_async_remote_copy(
            src_ref=ref.at[src],
            dst_ref=ref.at[dst],
            send_sem=halo_s.at[n],
            recv_sem=halo_r.at[n],
            device_id=device,
            device_id_type=MESH,
        )

    right, left = (r, lax.rem(c + 1, COLS)), (r, lax.rem(c + COLS - 1, COLS))
    up, down = (lax.rem(r + 1, ROWS), c), (lax.rem(r + ROWS - 1, ROWS), c)
    four = pl.ds(1, 4)
    x_halo, y_halo, corners = [], [], []
    for i, ref in enumerate((ext_c, ext_p)):
        x_halo.append(halo(8 * i + 0, ref, (four, 4), (four, 0), right))
        x_halo.append(halo(8 * i + 1, ref, (four, 1), (four, 5), left))
        y_halo.append(halo(8 * i + 2, ref, (4, four), (0, four), up))
        y_halo.append(halo(8 * i + 3, ref, (1, four), (5, four), down))
        corners.append(halo(8 * i + 4, ref, (4, 0), (0, 0), up))
        corners.append(halo(8 * i + 5, ref, (4, 5), (0, 5), up))
        corners.append(halo(8 * i + 6, ref, (1, 0), (5, 0), down))
        corners.append(halo(8 * i + 7, ref, (1, 5), (5, 5), down))
    for copy in x_halo + y_halo:
        copy.start()

    def to_col(k, src, ref, send, recv):
        return pltpu.make_async_remote_copy(
            src_ref=src,
            dst_ref=ref.at[c],
            send_sem=send.at[k],
            recv_sem=recv.at[k],
            device_id=(r, lax.rem(c + k, COLS)),
            device_id_type=MESH,
        )

    def to_row(k):
        return pltpu.make_async_remote_copy(
            src_ref=two_send,
            dst_ref=two_all.at[r],
            send_sem=two_s.at[k],
            recv_sem=two_r.at[k],
            device_id=(lax.rem(r + k, ROWS), c),
            device_id_type=MESH,
        )

    def couple_copies(k):
        return to_col(k, ctwo_send, ctwo_all, ctwo_s, ctwo_r), to_col(k, lists_send, lists_all, lt_s, lt_r)

    def start_couple(k, _):
        for copy in couple_copies(k):
            copy.start()
        return 0

    lax.fori_loop(1, COLS, start_couple, 0)
    ctwo_all[c] = ctwo_send[...]
    lists_all[c] = lists_send[...]

    for tile in range(32):
        b = basis[:, tile * 128 : tile * 128 + 128]
        zero = jnp.zeros((32, 64), BF16)
        split_basis[tile] = jnp.concatenate(
            [jnp.concatenate([b[:, :64], zero], axis=1), jnp.concatenate([zero, b[:, 64:]], axis=1)], axis=0
        )

    def lift(n, _):
        for i in range(4):
            lanes = pl.ds(pl.multiple_of(n * 512 + i * 128, 128), 128)
            coef[n, i * 64 : i * 64 + 64] = mm(split_basis[n * 4 + i], charges[:, lanes], NT).astype(BF16)
        field[n] = mm(t_one[n], coef[n], TN)
        return 0

    lax.fori_loop(0, 8, lift, 0)
    ones = [field[n].astype(BF16) for n in range(8)]
    for i in range(4):
        one_send[i] = jnp.concatenate([ones[2 * i], ones[2 * i + 1]], axis=1)
    two = mm(t_two[...], jnp.concatenate(ones, axis=0), TN).astype(BF16)
    two_send[...] = jnp.concatenate([two[:16], two[16:]], axis=1)

    def start_two(k, _):
        to_row(k).start()
        return 0

    def start_one(k, _):
        to_col(k, one_send, one_all, one_s, one_r).start()
        return 0

    lax.fori_loop(1, ROWS, start_two, 0)
    lax.fori_loop(1, COLS, start_one, 0)
    one_all[c] = one_send[...]
    one_all[COLS] = jnp.zeros((4, 32, 128), BF16)
    two_all[r] = two_send[...]
    two_all[ROWS] = jnp.zeros((16, 128), BF16)

    active = jnp.where(near_list[...] >= 0, 1.0, 0.0)
    lists = jnp.concatenate([active[:, 0:9], active[:, 9:18], active[:, 18:27]], axis=0).astype(BF16)
    blocked = jnp.where(mm(pick[...], lists) > 0.5, 0.0, jnp.inf)
    low2 = lax.broadcasted_iota(jnp.int32, (128, 128), 1) < 64
    for j in range(9):
        masks[j] = jnp.where(low2, blocked[0:128, j : j + 1], blocked[128:256, j : j + 1])

    coord = lax.broadcasted_iota(jnp.int32, (4, 256), 0)
    middle = jnp.where(coord == 0, 4 * c + 2, jnp.where(coord == 1, 4 * r + 2, jnp.where(coord == 2, 2, 0))).astype(F32)

    def prepare(y, x):
        p = ext_p[y, x] - middle
        q = p * p
        size = q[0:1] + q[1:2] + q[2:3]
        f = jnp.concatenate([-2.0 * p[0:3], size, jnp.zeros((4, 256), F32)], axis=0)
        e = y * 6 + x
        f0, f1 = f[:, :128], f[:, 128:]
        src_f[e, 0:8] = f0
        src_f[e, 8:16] = jnp.where(low[:8], f1, f0)
        src_f[e, 16:24] = f1
        ch = ext_c[y, x]
        c0, c1 = ch[:, :128], ch[:, 128:]
        zero = jnp.zeros((64, 64), BF16)
        wide_c[e, :, 0:128] = c0
        wide_c[e, :, 128:256] = jnp.concatenate([c1[:, :64], zero], axis=1)
        wide_c[e, :, 256:384] = c1
        wide_c[e, :, 384:512] = jnp.concatenate([zero, c0[:, 64:]], axis=1)
        return p, size

    def own_column(i, _):
        x, y = i // 4, lax.rem(i, 4)
        p, size = prepare(1 + y, 1 + x)
        features = (p[0:1], p[1:2], p[2:3], size + SOFT)
        for f, row in enumerate(features):
            for h in range(2):
                half = jnp.broadcast_to(row[:, h * 128 : h * 128 + 128], (128, 128))
                own_f[i, f, h * 128 : h * 128 + 128] = jnp.transpose(half)
            own_f[i, f, 256:320] = jnp.where(low, own_f[i, f, 64:128], own_f[i, f, 128:192])
        return 0

    lax.fori_loop(0, 16, own_column, 0)

    def unit(i):
        g, k = i // 4, lax.rem(i, 4)
        gx, gy, a, b = g // 2, lax.rem(g, 2), k // 2, lax.rem(k, 2)
        x = (1 - gx) * (1 + a) + gx * 3 * a
        y = (1 - gy) * (1 + b) + gy * 3 * b
        d = x * 4 + y
        total = [jnp.zeros((128, 64), F32), jnp.zeros((128, 64), F32)]
        zero = jnp.zeros((64, 128), BF16)
        for j in range(9):
            e = (y + j // 3) * 6 + x + j % 3
            rows = pl.ds(pl.multiple_of(d * 8, 8), 8)
            s0, sm, s1 = src_f[e, 0:8], src_f[e, 8:16], src_f[e, 16:24]
            m = masks[j, rows]

            def tile(t, first, s):
                dist = own_f[d, 3, first : first + 64] + (s[3:4] + m[t : t + 1])
                for f in range(3):
                    dist = dist + own_f[d, f, first : first + 64] * s[f : f + 1]
                return lax.rsqrt(dist.astype(BF16))

            mid = tile(2, 256, sm)
            k0 = jnp.concatenate(
                [jnp.concatenate([tile(0, 0, s0), zero], 1), jnp.concatenate([tile(1, 64, s0), mid], 1)], 0
            )
            k1 = jnp.concatenate(
                [jnp.concatenate([tile(3, 128, s1), mid], 1), jnp.concatenate([tile(4, 192, s1), zero], 1)], 0
            )
            total[0] = total[0] + mm(k0, wide_c[e, :, 0:256], NT)
            total[1] = total[1] + mm(k1, wide_c[e, :, 256:512], NT)
        near[d, :, 0:128] = jnp.transpose(total[0])
        near[d, :, 128:256] = jnp.transpose(total[1])

    def unit_step(i, _):
        unit(i)
        return 0

    lax.fori_loop(0, 4, unit_step, 0)

    for copy in x_halo:
        copy.wait()
    for copy in corners:
        copy.start()

    def wait_couple(k, _):
        for copy in couple_copies(k):
            copy.wait()
        return 0

    def wait_two(k, _):
        to_row(k).wait()
        return 0

    def wait_one(k, _):
        to_col(k, one_send, one_all, one_s, one_r).wait()
        return 0

    lax.fori_loop(1, COLS, wait_couple, 0)
    to_scalar = pltpu.make_async_copy(lists_all, lists_s, local)
    to_scalar.start()
    to_scalar.wait()
    lax.fori_loop(1, ROWS, wait_two, 0)

    def share(k, _):
        peer = lax.rem(c + k, COLS)
        for s in range(16):
            node = lists_s[peer, 0, s]
            at = jnp.where(lax.rem(node, COLS) == c, node // COLS, ROWS)
            v = two_all[at]
            chosen[s * 32 : s * 32 + 16] = v[:, :64]
            chosen[s * 32 + 16 : s * 32 + 32] = v[:, 64:]
        part = mm(ctwo_all[peer], chosen[...])
        part_send[k] = jnp.concatenate([part[:16], part[16:]], axis=1)
        return 0

    def part_copy(k):
        return to_col(k, part_send.at[k], part_all, part_s, part_r)

    def share_and_send(k, _):
        share(k, 0)
        part_copy(k).start()
        return 0

    lax.fori_loop(1, COLS, share_and_send, 0)
    share(0, 0)
    part_all[c] = part_send[0]

    lax.fori_loop(1, COLS, wait_one, 0)
    start = r * 64

    def couple(n, _):
        for s in range(12):
            node = list_one[n, s]
            p = jnp.clip(node - start, 0, 63)
            at = jnp.where(node >= 0, p // 8, COLS)
            v = one_all[at, lax.rem(p, 8) // 2]
            chosen[s * 32 : s * 32 + 32] = jnp.where(lax.rem(p, 2) == 1, v[:, 64:], v[:, :64])
        wide = jnp.concatenate([c_one[n, s] for s in range(12)], axis=1)
        field[n] = mm(wide, chosen[0:384])
        return 0

    lax.fori_loop(0, 8, couple, 0)

    for copy in y_halo:
        copy.wait()

    def beside(i, _):
        prepare(0, 1 + i)
        prepare(5, 1 + i)
        prepare(1 + i, 0)
        prepare(1 + i, 5)
        return 0

    lax.fori_loop(0, 4, beside, 0)
    lax.fori_loop(4, 12, unit_step, 0)
    for copy in corners:
        copy.wait()
    for y in (0, 5):
        for x in (0, 5):
            prepare(y, x)
    lax.fori_loop(12, 16, unit_step, 0)

    def wait_part(k, _):
        part_copy(k).wait()
        return 0

    lax.fori_loop(1, COLS, wait_part, 0)
    part = part_all[0]
    for k in range(1, COLS):
        part = part + part_all[k]
    top = jnp.concatenate([part[:, :64], part[:, 64:]], axis=0)
    top_high = top.astype(BF16)
    top_low = (top - top_high.astype(F32)).astype(BF16)

    def lower(n, _):
        rows = pl.ds(pl.multiple_of(n * 32, 32), 32)
        t = t_two[rows]
        one = field[n] + mm(t, top_high) + mm(t, top_low)
        high = one.astype(BF16)
        rest = (one - high.astype(F32)).astype(BF16)
        coef[n] = (mm(t_one[n], high) + mm(t_one[n], rest)).astype(BF16)
        return 0

    lax.fori_loop(0, 8, lower, 0)

    def finish(i, _):
        x1, y = i // 4, lax.rem(i, 4)
        even, odd = 2 * x1 * 4 + y, (2 * x1 + 1) * 4 + y
        for h in range(2):
            at = slice(h * 128, h * 128 + 128)
            a, b = near[even, :, at], near[odd, :, at]
            for z0 in range(2):
                tile = lax.rem(y, 2) + 2 * z0 + 4 * x1 + 8 * (y // 2) + 16 * h
                rows = pl.ds(pl.multiple_of(lax.rem(tile, 4) * 64, 64), 64)
                far = mm(coef[tile // 4, rows], split_basis[tile], TN)
                lanes = pl.ds(pl.multiple_of(tile * 128, 128), 128)
                out[:, lanes] = (halves(a, b, z0) * SCALE + far).astype(BF16)
        return 0

    lax.fori_loop(0, 8, finish, 0)


def shards(charges, points, leaf_basis, transfer_one, transfer_two, couple_one, couple_two, near_list, list_one, list_two):
    vmem = pl.BlockSpec(memory_space=pltpu.VMEM)
    smem = pl.BlockSpec(memory_space=pltpu.SMEM)
    dma = pltpu.SemaphoreType.DMA
    return pl.pallas_call(
        body,
        out_shape=jax.ShapeDtypeStruct(charges.shape, BF16),
        in_specs=[vmem] * 8 + [smem, vmem, vmem],
        out_specs=vmem,
        scratch_shapes=[
            pltpu.VMEM((6, 6, 64, 256), BF16),
            pltpu.VMEM((6, 6, 4, 256), F32),
            pltpu.VMEM((36, 64, 512), BF16),
            pltpu.VMEM((36, 24, 128), F32),
            pltpu.VMEM((16, 4, 320, 128), F32),
            pltpu.VMEM((9, 128, 128), F32),
            pltpu.VMEM((8, 128), F32),
            pltpu.VMEM((16, 64, 256), F32),
            pltpu.VMEM((32, 64, 128), BF16),
            pltpu.VMEM((8, 256, 64), BF16),
            pltpu.VMEM((4, 32, 128), BF16),
            pltpu.VMEM((9, 4, 32, 128), BF16),
            pltpu.VMEM((16, 128), BF16),
            pltpu.VMEM((33, 16, 128), BF16),
            pltpu.VMEM((32, 512), BF16),
            pltpu.VMEM((8, 32, 512), BF16),
            pltpu.VMEM((8, 128), jnp.int32),
            pltpu.VMEM((8, 8, 128), jnp.int32),
            pltpu.SMEM((8, 8, 128), jnp.int32),
            pltpu.VMEM((512, 64), BF16),
            pltpu.VMEM((8, 32, 64), F32),
            pltpu.VMEM((8, 16, 128), F32),
            pltpu.VMEM((8, 16, 128), F32),
            dma((16,)),
            dma((16,)),
            dma((COLS,)),
            dma((COLS,)),
            dma((ROWS,)),
            dma((ROWS,)),
            dma((COLS,)),
            dma((COLS,)),
            dma((COLS,)),
            dma((COLS,)),
            dma((COLS,)),
            dma((COLS,)),
            dma,
        ],
        compiler_params=pltpu.CompilerParams(
            collective_id=0, has_side_effects=True, vmem_limit_bytes=58 * 2**20
        ),
    )(
        charges,
        points,
        leaf_basis,
        transfer_one.reshape(8, 256, 32),
        transfer_two.reshape(256, 32),
        couple_one,
        couple_two.reshape(16, 32, 32),
        near_list,
        list_one,
        list_two,
        jnp.asarray(picks(), BF16),
    )


def solution(mesh):
    lead = ("row", "col")
    columns, three = P(None, lead), P(lead, None, None)
    four, two = P(lead, None, None, None), P(lead, None)
    in_specs = (columns, columns, columns, three, three, four, four, two, two, two)
    return jax.shard_map(shards, mesh=mesh, in_specs=in_specs, out_specs=columns, check_vma=False)
```

time: 441 us -> 59.4 us (0.13)
  local copies, waits for them, and re-layouts: 238 us -> 5.73 us
  other arithmetic: 82 us -> 0 us
  starting transfers between devices: 53.9 us -> 0 us
  Pallas kernels: 0 us -> 53.4 us
  matrix products: 49.2 us -> 0 us
  loops' own time: 13.2 us -> 0 us
    while x224 -> x0, local copies, waits for them, and re-layouts: 137 us -> none
    reduce_sum x4 -> x0, other arithmetic: 74.7 us -> none  [leaf_block(): jnp.sum(distance * distance, axis=2) + softening]
    reshape x12 -> x0, local copies, waits for them, and re-layouts: 53.9 us -> none  [the longest x4 43.7 us: near_step(): jnp.stack(value_list, axis=2).reshape(block_leaves, 27, rhs_count, per_leaf)]
    pallas_call x0 -> x1, Pallas kernels: none -> 53.4 us  [shards(): pl.pallas_call(body, out_shape=jax.ShapeDtypeStruct(charges.shape, BF16),...]
    dot_general x11 -> x0, matrix products: 49.2 us -> none  [the longest x4 40.7 us: leaf_block(): jnp.einsum('lsij,lsrj->lri', kernel, values, preferred_element_type=jnp.f...]
    all_to_all x3 -> x0, starting transfers between devices: 29.3 us -> none  [sent_to_all(): lax.all_to_all(jnp.broadcast_to(value[None], (devices, *value.shape)), ax...]
    ppermute x8 -> x0, starting transfers between devices: 24.5 us -> none  [the longest x4 18.1 us: padded(): before = lax.ppermute(last, axis, up)]
    another operation x1 -> x0, loops' own time: 13.2 us -> none  [shards(): near_layers = lax.map(near_step, jnp.arange(depth_z, dtype=jnp.int32))]
  transfers between devices with their start and end apart: 11 -> 0, of which waited for: 0 -> 0; matrix products, arithmetic and copies ran while one was open for 80% -> 0% of each run, Pallas kernels for 0% -> 0%
where the time goes in v1:
time: 59.4 us; the launch traced here: 59.2 us
  Pallas kernels  53.4 us (90%)
  local copies, waits for them, and re-layouts  5.73 us (10%)
    pallas_call x1, Pallas kernels, shards(): pl.pallas_call(body, out_shape=jax.ShapeDtypeStruct(charges.shape, BF16),...  53.4 us
    unnamed x3, local copies, waits for them, and re-layouts  5.73 us

profile of v1, /device:TPU:1, one launch (start us, length us, event | category | flops | bytes accessed | tf_op | source)
XLA Modules:
  0.0 59.2 jit_solution(5565695493592992139)
XLA Ops:
  0.0 1.4 %copy.13.near_list = s32[64,27]{1,0:T(8,128)} copy(s32[64,27]{0,1:T(8,128)} %param.18) | data formatting | bytes 13824 | tf_op args[7]
  1.4 2.5 %copy.12 = bf16[64,32,32]{2,1,0:T(8,128)(2,1)} copy(bf16[64,32,32]{0,2,1:T(8,128)(2,1)} %param.14) | data formatting | bytes 262144 | tf_op args[3]
  3.9 53.4 %shard_map.109 = bf16[64,4096]{1,0:T(8,128)(2,1)} custom-call(bf16[64,4096]{1,0:T(8,128)(2,1)} %charges.1, f32[3,4096]{1,0:T(4,128)} %points.1, bf16[32,4096]{1,0:T(8,128)(2,1)} %basis.1, bf16[8,256,32]{2,1,0:T(8,128)(2,1)} %bitcast.3, bf16[256,32]{1,0:T(8,128)(2,1)} %bitcast.5, bf16[8,12,32,32]{3,2,1,0:T(8,128)(2,1)} %c_one.1, bf16[16,32,32]{2,1,0:T(8,128)(2,1)} %bitcast.4, ...), custom_call_target="tpu_custom_call" | custom-call | tf_op jit(solution)/shard_map/pallas_call | solution.py:435
  57.3 1.9 %copy.15 = bf16[64,4096]{1,0:T(8,128)(2,1)} copy(bf16[64,4096]{1,0:T(8,128)(2,1)} %shard_map.109) | data formatting | bytes 1048576

commit v2 on v1

--- a/solution.py
+++ b/solution.py
@@ -123,7 +123,7 @@
                 ext_p[1 + y, 1 + 2 * x1 + x0, 3:4, at] = jnp.zeros((1, 128), F32)
         return 0
 
-    lax.fori_loop(0, 8, arrange, 0)
+    lax.fori_loop(0, 8, arrange, 0, unroll=True)
 
     ctwo_send[...] = jnp.concatenate([c_two[s] for s in range(16)], axis=1)
     lists_send[...] = jnp.zeros_like(lists_send)
@@ -154,7 +154,7 @@
         corners.append(halo(8 * i + 5, ref, (4, 5), (0, 5), up))
         corners.append(halo(8 * i + 6, ref, (1, 0), (5, 0), down))
         corners.append(halo(8 * i + 7, ref, (1, 5), (5, 5), down))
-    for copy in x_halo + y_halo:
+    for copy in y_halo:
         copy.start()
 
     def to_col(k, src, ref, send, recv):
@@ -186,6 +186,8 @@
         return 0
 
     lax.fori_loop(1, COLS, start_couple, 0)
+    for copy in x_halo:
+        copy.start()
     ctwo_all[c] = ctwo_send[...]
     lists_all[c] = lists_send[...]
 
@@ -203,7 +205,7 @@
         field[n] = mm(t_one[n], coef[n], TN)
         return 0
 
-    lax.fori_loop(0, 8, lift, 0)
+    lax.fori_loop(0, 8, lift, 0, unroll=True)
     ones = [field[n].astype(BF16) for n in range(8)]
     for i in range(4):
         one_send[i] = jnp.concatenate([ones[2 * i], ones[2 * i + 1]], axis=1)
@@ -225,7 +227,7 @@
     two_all[r] = two_send[...]
     two_all[ROWS] = jnp.zeros((16, 128), BF16)
 
-    active = jnp.where(near_list[...] >= 0, 1.0, 0.0)
+    active = jnp.transpose(jnp.where(near_list[...] >= 0, 1.0, 0.0))
     lists = jnp.concatenate([active[:, 0:9], active[:, 9:18], active[:, 18:27]], axis=0).astype(BF16)
     blocked = jnp.where(mm(pick[...], lists) > 0.5, 0.0, jnp.inf)
     low2 = lax.broadcasted_iota(jnp.int32, (128, 128), 1) < 64
@@ -265,7 +267,7 @@
             own_f[i, f, 256:320] = jnp.where(low, own_f[i, f, 64:128], own_f[i, f, 128:192])
         return 0
 
-    lax.fori_loop(0, 16, own_column, 0)
+    lax.fori_loop(0, 16, own_column, 0, unroll=2)
 
     def unit(i):
         g, k = i // 4, lax.rem(i, 4)
@@ -305,10 +307,16 @@
 
     lax.fori_loop(0, 4, unit_step, 0)
 
-    for copy in x_halo:
+    for copy in y_halo:
         copy.wait()
-    for copy in corners:
-        copy.start()
+
+    def beside_y(i, _):
+        prepare(0, 1 + i)
+        prepare(5, 1 + i)
+        return 0
+
+    lax.fori_loop(0, 4, beside_y, 0, unroll=True)
+    lax.fori_loop(4, 8, unit_step, 0)
 
     def wait_couple(k, _):
         for copy in couple_copies(k):
@@ -349,7 +357,7 @@
         part_copy(k).start()
         return 0
 
-    lax.fori_loop(1, COLS, share_and_send, 0)
+    lax.fori_loop(1, COLS, share_and_send, 0, unroll=True)
     share(0, 0)
     part_all[c] = part_send[0]
 
@@ -367,26 +375,20 @@
         field[n] = mm(wide, chosen[0:384])
         return 0
 
-    lax.fori_loop(0, 8, couple, 0)
-
-    for copy in y_halo:
+    lax.fori_loop(0, 8, couple, 0, unroll=True)
+
+    for copy in x_halo:
         copy.wait()
-
-    def beside(i, _):
-        prepare(0, 1 + i)
-        prepare(5, 1 + i)
+    for copy in corners:
+        copy.start()
+
+    def beside_x(i, _):
         prepare(1 + i, 0)
         prepare(1 + i, 5)
         return 0
 
-    lax.fori_loop(0, 4, beside, 0)
-    lax.fori_loop(4, 12, unit_step, 0)
-    for copy in corners:
-        copy.wait()
-    for y in (0, 5):
-        for x in (0, 5):
-            prepare(y, x)
-    lax.fori_loop(12, 16, unit_step, 0)
+    lax.fori_loop(0, 4, beside_x, 0, unroll=True)
+    lax.fori_loop(8, 12, unit_step, 0)
 
     def wait_part(k, _):
         part_copy(k).wait()
@@ -409,7 +411,7 @@
         coef[n] = (mm(t_one[n], high) + mm(t_one[n], rest)).astype(BF16)
         return 0
 
-    lax.fori_loop(0, 8, lower, 0)
+    lax.fori_loop(0, 8, lower, 0, unroll=True)
 
     def finish(i, _):
         x1, y = i // 4, lax.rem(i, 4)
@@ -425,7 +427,13 @@
                 out[:, lanes] = (halves(a, b, z0) * SCALE + far).astype(BF16)
         return 0
 
-    lax.fori_loop(0, 8, finish, 0)
+    for copy in corners:
+        copy.wait()
+    for y in (0, 5):
+        for x in (0, 5):
+            prepare(y, x)
+    lax.fori_loop(12, 16, unit_step, 0)
+    lax.fori_loop(0, 8, finish, 0, unroll=True)
 
 
 def shards(charges, points, leaf_basis, transfer_one, transfer_two, couple_one, couple_two, near_list, list_one, list_two):
@@ -486,7 +494,7 @@
         transfer_two.reshape(256, 32),
         couple_one,
         couple_two.reshape(16, 32, 32),
-        near_list,
+        near_list.T,
         list_one,
         list_two,
         jnp.asarray(picks(), BF16),

time: 59.4 us -> 52.4 us (0.88)
  Pallas kernels: 53.4 us -> 47.9 us
  local copies, waits for them, and re-layouts: 5.73 us -> 4.32 us
    pallas_call x1, Pallas kernels: 53.4 us -> 47.9 us  [shards(): pl.pallas_call(body, out_shape=jax.ShapeDtypeStruct(charges.shape, BF16),...]
    unnamed x3 -> x2, local copies, waits for them, and re-layouts: 5.73 us -> 4.32 us
where the time goes in v2:
time: 52.4 us; the launch traced here: 52.2 us
  Pallas kernels  47.9 us (91%)
  local copies, waits for them, and re-layouts  4.32 us (8%)
    pallas_call x1, Pallas kernels, shards(): pl.pallas_call(body, out_shape=jax.ShapeDtypeStruct(charges.shape, BF16),...  47.9 us
    unnamed x2, local copies, waits for them, and re-layouts  4.32 us

profile of v2, /device:TPU:1, one launch (start us, length us, event | category | flops | bytes accessed | tf_op | source)
XLA Modules:
  0.0 52.2 jit_solution(9319342106462368426)
XLA Ops:
  0.0 2.5 %copy.12 = bf16[64,32,32]{2,1,0:T(8,128)(2,1)} copy(bf16[64,32,32]{0,2,1:T(8,128)(2,1)} %param.14) | data formatting | bytes 262144 | tf_op args[3]
  2.5 47.9 %shard_map.109 = bf16[64,4096]{1,0:T(8,128)(2,1)} custom-call(bf16[64,4096]{1,0:T(8,128)(2,1)} %charges.1, f32[3,4096]{1,0:T(4,128)} %points.1, bf16[32,4096]{1,0:T(8,128)(2,1)} %basis.1, bf16[8,256,32]{2,1,0:T(8,128)(2,1)} %bitcast.4, bf16[256,32]{1,0:T(8,128)(2,1)} %bitcast.6, bf16[8,12,32,32]{3,2,1,0:T(8,128)(2,1)} %c_one.1, bf16[16,32,32]{2,1,0:T(8,128)(2,1)} %bitcast.5, ...), custom_call_target="tpu_custom_call" | custom-call | tf_op jit(solution)/shard_map/pallas_call | solution.py:443
  50.3 1.9 %copy.14 = bf16[64,4096]{1,0:T(8,128)(2,1)} copy(bf16[64,4096]{1,0:T(8,128)(2,1)} %shard_map.109) | data formatting | bytes 1048576

commit v3 on v2

--- a/solution.py
+++ b/solution.py
@@ -40,7 +40,7 @@
     charges,
     points,
     basis,
-    t_one,
+    t_packed,
     t_two,
     c_one,
     c_two,
@@ -55,7 +55,8 @@
     src_f,
     own_f,
     masks,
-    shifted,
+    t_flat,
+    t_one,
     near,
     split_basis,
     coef,
@@ -94,12 +95,23 @@
         pl.semaphore_signal(barrier, inc=1, device_id=(r, lax.rem(c + k, COLS)), device_id_type=MESH)
         return 0
 
-    def greet_row(k, _):
-        pl.semaphore_signal(barrier, inc=1, device_id=(lax.rem(r + k, ROWS), c), device_id_type=MESH)
+    layer, spot = r // 4, lax.rem(r, 4)
+
+    def quad_peer(k):
+        return (layer * 4 + lax.rem(spot + k, 4), c)
+
+    def ring_peer(k):
+        return (lax.rem(layer + k, 8) * 4 + spot, c)
+
+    def greet_ring(k, _):
+        pl.semaphore_signal(barrier, inc=1, device_id=ring_peer(k), device_id_type=MESH)
         return 0
 
     lax.fori_loop(1, COLS, greet_col, 0)
-    lax.fori_loop(1, ROWS, greet_row, 0)
+    lax.fori_loop(1, 8, greet_ring, 0)
+    up, down = (lax.rem(r + 1, ROWS), c), (lax.rem(r + ROWS - 1, ROWS), c)
+    for peer in (quad_peer(1), quad_peer(2), quad_peer(3), up, down):
+        pl.semaphore_signal(barrier, inc=1, device_id=peer, device_id_type=MESH)
 
     low = lax.broadcasted_iota(jnp.int32, (64, 128), 1) < 64
 
@@ -129,7 +141,7 @@
     lists_send[...] = jnp.zeros_like(lists_send)
     lists_send[0:1, 0:16] = list_two[...]
 
-    pl.semaphore_wait(barrier, COLS + ROWS - 2)
+    pl.semaphore_wait(barrier, COLS - 1 + 7 + 5)
 
     def halo(n, ref, src, dst, device):
         return pltpu.make_async_remote_copy(
@@ -142,7 +154,6 @@
         )
 
     right, left = (r, lax.rem(c + 1, COLS)), (r, lax.rem(c + COLS - 1, COLS))
-    up, down = (lax.rem(r + 1, ROWS), c), (lax.rem(r + ROWS - 1, ROWS), c)
     four = pl.ds(1, 4)
     x_halo, y_halo, corners = [], [], []
     for i, ref in enumerate((ext_c, ext_p)):
@@ -167,13 +178,24 @@
             device_id_type=MESH,
         )
 
-    def to_row(k):
+    def to_quad(k):
         return pltpu.make_async_remote_copy(
             src_ref=two_send,
             dst_ref=two_all.at[r],
             send_sem=two_s.at[k],
             recv_sem=two_r.at[k],
-            device_id=(lax.rem(r + k, ROWS), c),
+            device_id=quad_peer(k),
+            device_id_type=MESH,
+        )
+
+    def to_ring(k):
+        quad = two_all.at[pl.ds(layer * 4, 4)]
+        return pltpu.make_async_remote_copy(
+            src_ref=quad,
+            dst_ref=quad,
+            send_sem=two_s.at[4 + k],
+            recv_sem=two_r.at[4 + k],
+            device_id=ring_peer(k),
             device_id_type=MESH,
         )
 
@@ -186,10 +208,15 @@
         return 0
 
     lax.fori_loop(1, COLS, start_couple, 0)
-    for copy in x_halo:
-        copy.start()
     ctwo_all[c] = ctwo_send[...]
     lists_all[c] = lists_send[...]
+
+    for a in range(0, 32, 4):
+        turned = jnp.transpose(t_packed[a * 32 : a * 32 + 128].astype(F32))
+        for q in range(4):
+            t_flat[pl.ds(a + q, 64, stride=32)] = turned[:, q * 32 : q * 32 + 32]
+    for n in range(8):
+        t_one[n] = t_flat[n * 256 : n * 256 + 256].astype(BF16)
 
     for tile in range(32):
         b = basis[:, tile * 128 : tile * 128 + 128]
@@ -212,16 +239,19 @@
     two = mm(t_two[...], jnp.concatenate(ones, axis=0), TN).astype(BF16)
     two_send[...] = jnp.concatenate([two[:16], two[16:]], axis=1)
 
-    def start_two(k, _):
-        to_row(k).start()
+    def start_ring(k, _):
+        to_ring(k).start()
         return 0
 
     def start_one(k, _):
         to_col(k, one_send, one_all, one_s, one_r).start()
         return 0
 
-    lax.fori_loop(1, ROWS, start_two, 0)
+    for k in (1, 2, 3):
+        to_quad(k).start()
     lax.fori_loop(1, COLS, start_one, 0)
+    for copy in x_halo:
+        copy.start()
     one_all[c] = one_send[...]
     one_all[COLS] = jnp.zeros((4, 32, 128), BF16)
     two_all[r] = two_send[...]
@@ -305,6 +335,9 @@
         unit(i)
         return 0
 
+    for k in (1, 2, 3):
+        to_quad(k).wait()
+    lax.fori_loop(1, 8, start_ring, 0)
     lax.fori_loop(0, 4, unit_step, 0)
 
     for copy in y_halo:
@@ -323,8 +356,8 @@
             copy.wait()
         return 0
 
-    def wait_two(k, _):
-        to_row(k).wait()
+    def wait_ring(k, _):
+        to_ring(k).wait()
         return 0
 
     def wait_one(k, _):
@@ -335,7 +368,7 @@
     to_scalar = pltpu.make_async_copy(lists_all, lists_s, local)
     to_scalar.start()
     to_scalar.wait()
-    lax.fori_loop(1, ROWS, wait_two, 0)
+    lax.fori_loop(1, 8, wait_ring, 0)
 
     def share(k, _):
         peer = lax.rem(c + k, COLS)
@@ -452,7 +485,8 @@
             pltpu.VMEM((36, 24, 128), F32),
             pltpu.VMEM((16, 4, 320, 128), F32),
             pltpu.VMEM((9, 128, 128), F32),
-            pltpu.VMEM((8, 128), F32),
+            pltpu.VMEM((2048, 32), F32),
+            pltpu.VMEM((8, 256, 32), BF16),
             pltpu.VMEM((16, 64, 256), F32),
             pltpu.VMEM((32, 64, 128), BF16),
             pltpu.VMEM((8, 256, 64), BF16),
@@ -473,8 +507,8 @@
             dma((16,)),
             dma((COLS,)),
             dma((COLS,)),
-            dma((ROWS,)),
-            dma((ROWS,)),
+            dma((12,)),
+            dma((12,)),
             dma((COLS,)),
             dma((COLS,)),
             dma((COLS,)),
@@ -490,7 +524,7 @@
         charges,
         points,
         leaf_basis,
-        transfer_one.reshape(8, 256, 32),
+        transfer_one.transpose(1, 2, 0).reshape(1024, 64),
         transfer_two.reshape(256, 32),
         couple_one,
         couple_two.reshape(16, 32, 32),

time: 52.4 us -> 52.3 us (level)
  local copies, waits for them, and re-layouts: 4.32 us -> 1.87 us
  Pallas kernels: 47.9 us -> 50.3 us
    unnamed x2 -> x1, local copies, waits for them, and re-layouts: 4.32 us -> 1.87 us
    pallas_call x1, Pallas kernels: 47.9 us -> 50.3 us  [shards(): pl.pallas_call(body, out_shape=jax.ShapeDtypeStruct(charges.shape, BF16),...]
where the time goes in v3:
time: 52.3 us; the launch traced here: 52.2 us
  Pallas kernels  50.3 us (96%)
  local copies, waits for them, and re-layouts  1.87 us (4%)
    pallas_call x1, Pallas kernels, shards(): pl.pallas_call(body, out_shape=jax.ShapeDtypeStruct(charges.shape, BF16),...  50.3 us
    unnamed x1, local copies, waits for them, and re-layouts  1.87 us

profile of v3, /device:TPU:1, one launch (start us, length us, event | category | flops | bytes accessed | tf_op | source)
XLA Modules:
  0.0 52.2 jit_solution(622639227299833013)
XLA Ops:
  0.0 50.3 %shard_map.109 = bf16[64,4096]{1,0:T(8,128)(2,1)} custom-call(bf16[64,4096]{1,0:T(8,128)(2,1)} %charges.1, f32[3,4096]{1,0:T(4,128)} %points.1, bf16[32,4096]{1,0:T(8,128)(2,1)} %basis.1, bf16[1024,64]{1,0:T(8,128)(2,1)} %bitcast.6, bf16[256,32]{1,0:T(8,128)(2,1)} %bitcast.8, bf16[8,12,32,32]{3,2,1,0:T(8,128)(2,1)} %c_one.1, bf16[16,32,32]{2,1,0:T(8,128)(2,1)} %bitcast.7, ...), custom_call_target="tpu_custom_call" | custom-call | tf_op jit(solution)/shard_map/pallas_call | solution.py:476
  50.3 1.9 %copy.13 = bf16[64,4096]{1,0:T(8,128)(2,1)} copy(bf16[64,4096]{1,0:T(8,128)(2,1)} %shard_map.109) | data formatting | bytes 1048576

commit v4 on v3

--- a/solution.py
+++ b/solution.py
@@ -60,13 +60,10 @@
     near,
     split_basis,
     coef,
-    one_send,
     one_all,
     two_send,
     two_all,
-    ctwo_send,
     ctwo_all,
-    lists_send,
     lists_all,
     lists_s,
     chosen,
@@ -137,9 +134,9 @@
 
     lax.fori_loop(0, 8, arrange, 0, unroll=True)
 
-    ctwo_send[...] = jnp.concatenate([c_two[s] for s in range(16)], axis=1)
-    lists_send[...] = jnp.zeros_like(lists_send)
-    lists_send[0:1, 0:16] = list_two[...]
+    ctwo_all[c] = jnp.concatenate([c_two[s] for s in range(16)], axis=1)
+    lists_all[c] = jnp.zeros((8, 128), jnp.int32)
+    lists_all[c, 0:1, 0:16] = list_two[...]
 
     pl.semaphore_wait(barrier, COLS - 1 + 7 + 5)
 
@@ -165,8 +162,6 @@
         corners.append(halo(8 * i + 5, ref, (4, 5), (0, 5), up))
         corners.append(halo(8 * i + 6, ref, (1, 0), (5, 0), down))
         corners.append(halo(8 * i + 7, ref, (1, 5), (5, 5), down))
-    for copy in y_halo:
-        copy.start()
 
     def to_col(k, src, ref, send, recv):
         return pltpu.make_async_remote_copy(
@@ -199,17 +194,36 @@
             device_id_type=MESH,
         )
 
-    def couple_copies(k):
-        return to_col(k, ctwo_send, ctwo_all, ctwo_s, ctwo_r), to_col(k, lists_send, lists_all, lt_s, lt_r)
-
-    def start_couple(k, _):
-        for copy in couple_copies(k):
-            copy.start()
-        return 0
-
-    lax.fori_loop(1, COLS, start_couple, 0)
-    ctwo_all[c] = ctwo_send[...]
-    lists_all[c] = lists_send[...]
+    far_y = c + 1 - 2 * lax.rem(c, 2)
+    place = c // 2
+
+    def across(ref, send, recv):
+        return pltpu.make_async_remote_copy(
+            src_ref=ref.at[c],
+            dst_ref=ref.at[c],
+            send_sem=send.at[0],
+            recv_sem=recv.at[0],
+            device_id=(r, far_y),
+            device_id_type=MESH,
+        )
+
+    def along(k, ref, send, recv):
+        both = ref.at[pl.ds(place * 2, 2)]
+        return pltpu.make_async_remote_copy(
+            src_ref=both,
+            dst_ref=both,
+            send_sem=send.at[k],
+            recv_sem=recv.at[k],
+            device_id=(r, lax.rem(place + k, 4) * 2 + lax.rem(c, 2)),
+            device_id_type=MESH,
+        )
+
+    gathers = ((ctwo_all, ctwo_s, ctwo_r), (lists_all, lt_s, lt_r), (one_all, one_s, one_r))
+
+    for gather in gathers[:2]:
+        across(*gather).start()
+    for copy in y_halo + x_halo:
+        copy.start()
 
     for a in range(0, 32, 4):
         turned = jnp.transpose(t_packed[a * 32 : a * 32 + 128].astype(F32))
@@ -235,7 +249,7 @@
     lax.fori_loop(0, 8, lift, 0, unroll=True)
     ones = [field[n].astype(BF16) for n in range(8)]
     for i in range(4):
-        one_send[i] = jnp.concatenate([ones[2 * i], ones[2 * i + 1]], axis=1)
+        one_all[c, i] = jnp.concatenate([ones[2 * i], ones[2 * i + 1]], axis=1)
     two = mm(t_two[...], jnp.concatenate(ones, axis=0), TN).astype(BF16)
     two_send[...] = jnp.concatenate([two[:16], two[16:]], axis=1)
 
@@ -243,16 +257,13 @@
         to_ring(k).start()
         return 0
 
-    def start_one(k, _):
-        to_col(k, one_send, one_all, one_s, one_r).start()
-        return 0
-
     for k in (1, 2, 3):
         to_quad(k).start()
-    lax.fori_loop(1, COLS, start_one, 0)
-    for copy in x_halo:
-        copy.start()
-    one_all[c] = one_send[...]
+    across(*gathers[2]).start()
+    for gather in gathers[:2]:
+        across(*gather).wait()
+        for k in (1, 2, 3):
+            along(k, *gather).start()
     one_all[COLS] = jnp.zeros((4, 32, 128), BF16)
     two_all[r] = two_send[...]
     two_all[ROWS] = jnp.zeros((16, 128), BF16)
@@ -338,6 +349,9 @@
     for k in (1, 2, 3):
         to_quad(k).wait()
     lax.fori_loop(1, 8, start_ring, 0)
+    across(*gathers[2]).wait()
+    for k in (1, 2, 3):
+        along(k, *gathers[2]).start()
     lax.fori_loop(0, 4, unit_step, 0)
 
     for copy in y_halo:
@@ -351,20 +365,13 @@
     lax.fori_loop(0, 4, beside_y, 0, unroll=True)
     lax.fori_loop(4, 8, unit_step, 0)
 
-    def wait_couple(k, _):
-        for copy in couple_copies(k):
-            copy.wait()
-        return 0
-
     def wait_ring(k, _):
         to_ring(k).wait()
         return 0
 
-    def wait_one(k, _):
-        to_col(k, one_send, one_all, one_s, one_r).wait()
-        return 0
-
-    lax.fori_loop(1, COLS, wait_couple, 0)
+    for gather in gathers[:2]:
+        for k in (1, 2, 3):
+            along(k, *gather).wait()
     to_scalar = pltpu.make_async_copy(lists_all, lists_s, local)
     to_scalar.start()
     to_scalar.wait()
@@ -394,7 +401,8 @@
     share(0, 0)
     part_all[c] = part_send[0]
 
-    lax.fori_loop(1, COLS, wait_one, 0)
+    for k in (1, 2, 3):
+        along(k, *gathers[2]).wait()
     start = r * 64
 
     def couple(n, _):
@@ -490,13 +498,10 @@
             pltpu.VMEM((16, 64, 256), F32),
             pltpu.VMEM((32, 64, 128), BF16),
             pltpu.VMEM((8, 256, 64), BF16),
-            pltpu.VMEM((4, 32, 128), BF16),
             pltpu.VMEM((9, 4, 32, 128), BF16),
             pltpu.VMEM((16, 128), BF16),
             pltpu.VMEM((33, 16, 128), BF16),
-            pltpu.VMEM((32, 512), BF16),
             pltpu.VMEM((8, 32, 512), BF16),
-            pltpu.VMEM((8, 128), jnp.int32),
             pltpu.VMEM((8, 8, 128), jnp.int32),
             pltpu.SMEM((8, 8, 128), jnp.int32),
             pltpu.VMEM((512, 64), BF16),

time: 52.3 us -> 50.5 us (0.966)
  Pallas kernels: 50.3 us -> 48.5 us
    pallas_call x1, Pallas kernels: 50.3 us -> 48.5 us  [shards(): pl.pallas_call(body, out_shape=jax.ShapeDtypeStruct(charges.shape, BF16),...]
where the time goes in v4:
time: 50.5 us; the launch traced here: 50.4 us
  Pallas kernels  48.5 us (96%)
  local copies, waits for them, and re-layouts  1.87 us (4%)
    pallas_call x1, Pallas kernels, shards(): pl.pallas_call(body, out_shape=jax.ShapeDtypeStruct(charges.shape, BF16),...  48.5 us
    unnamed x1, local copies, waits for them, and re-layouts  1.87 us

profile of v4, /device:TPU:1, one launch (start us, length us, event | category | flops | bytes accessed | tf_op | source)
XLA Modules:
  0.0 50.4 jit_solution(11802695992477911152)
XLA Ops:
  0.0 48.5 %shard_map.109 = bf16[64,4096]{1,0:T(8,128)(2,1)} custom-call(bf16[64,4096]{1,0:T(8,128)(2,1)} %charges.1, f32[3,4096]{1,0:T(4,128)} %points.1, bf16[32,4096]{1,0:T(8,128)(2,1)} %basis.1, bf16[1024,64]{1,0:T(8,128)(2,1)} %bitcast.6, bf16[256,32]{1,0:T(8,128)(2,1)} %bitcast.8, bf16[8,12,32,32]{3,2,1,0:T(8,128)(2,1)} %c_one.1, bf16[16,32,32]{2,1,0:T(8,128)(2,1)} %bitcast.7, ...), custom_call_target="tpu_custom_call" | custom-call | tf_op jit(solution)/shard_map/pallas_call | solution.py:484
  48.5 1.9 %copy.13 = bf16[64,4096]{1,0:T(8,128)(2,1)} copy(bf16[64,4096]{1,0:T(8,128)(2,1)} %shard_map.109) | data formatting | bytes 1048576

commit v5 on v4

--- a/solution.py
+++ b/solution.py
@@ -138,8 +138,6 @@
     lists_all[c] = jnp.zeros((8, 128), jnp.int32)
     lists_all[c, 0:1, 0:16] = list_two[...]
 
-    pl.semaphore_wait(barrier, COLS - 1 + 7 + 5)
-
     def halo(n, ref, src, dst, device):
         return pltpu.make_async_remote_copy(
             src_ref=ref.at[src],
@@ -220,11 +218,6 @@
 
     gathers = ((ctwo_all, ctwo_s, ctwo_r), (lists_all, lt_s, lt_r), (one_all, one_s, one_r))
 
-    for gather in gathers[:2]:
-        across(*gather).start()
-    for copy in y_halo + x_halo:
-        copy.start()
-
     for a in range(0, 32, 4):
         turned = jnp.transpose(t_packed[a * 32 : a * 32 + 128].astype(F32))
         for q in range(4):
@@ -257,13 +250,13 @@
         to_ring(k).start()
         return 0
 
+    pl.semaphore_wait(barrier, COLS - 1 + 7 + 5)
     for k in (1, 2, 3):
         to_quad(k).start()
-    across(*gathers[2]).start()
-    for gather in gathers[:2]:
-        across(*gather).wait()
-        for k in (1, 2, 3):
-            along(k, *gather).start()
+    for gather in gathers:
+        across(*gather).start()
+    for copy in y_halo:
+        copy.start()
     one_all[COLS] = jnp.zeros((4, 32, 128), BF16)
     two_all[r] = two_send[...]
     two_all[ROWS] = jnp.zeros((16, 128), BF16)
@@ -349,9 +342,12 @@
     for k in (1, 2, 3):
         to_quad(k).wait()
     lax.fori_loop(1, 8, start_ring, 0)
-    across(*gathers[2]).wait()
-    for k in (1, 2, 3):
-        along(k, *gathers[2]).start()
+    for gather in gathers:
+        across(*gather).wait()
+        for k in (1, 2, 3):
+            along(k, *gather).start()
+    for copy in x_halo:
+        copy.start()
     lax.fori_loop(0, 4, unit_step, 0)
 
     for copy in y_halo:

time: 50.5 us -> 42.7 us (0.85)
  Pallas kernels: 48.5 us -> 40.7 us
    pallas_call x1, Pallas kernels: 48.5 us -> 40.7 us  [shards(): pl.pallas_call(body, out_shape=jax.ShapeDtypeStruct(charges.shape, BF16),...]
where the time goes in v5:
time: 42.7 us; the launch traced here: 42.5 us
  Pallas kernels  40.7 us (95%)
  local copies, waits for them, and re-layouts  1.87 us (4%)
    pallas_call x1, Pallas kernels, shards(): pl.pallas_call(body, out_shape=jax.ShapeDtypeStruct(charges.shape, BF16),...  40.7 us
    unnamed x1, local copies, waits for them, and re-layouts  1.87 us

profile of v5, /device:TPU:1, one launch (start us, length us, event | category | flops | bytes accessed | tf_op | source)
XLA Modules:
  0.0 42.5 jit_solution(2554806548671978674)
XLA Ops:
  0.0 40.7 %shard_map.109 = bf16[64,4096]{1,0:T(8,128)(2,1)} custom-call(bf16[64,4096]{1,0:T(8,128)(2,1)} %charges.1, f32[3,4096]{1,0:T(4,128)} %points.1, bf16[32,4096]{1,0:T(8,128)(2,1)} %basis.1, bf16[1024,64]{1,0:T(8,128)(2,1)} %bitcast.6, bf16[256,32]{1,0:T(8,128)(2,1)} %bitcast.8, bf16[8,12,32,32]{3,2,1,0:T(8,128)(2,1)} %c_one.1, bf16[16,32,32]{2,1,0:T(8,128)(2,1)} %bitcast.7, ...), custom_call_target="tpu_custom_call" | custom-call | tf_op jit(solution)/shard_map/pallas_call | solution.py:480
  40.7 1.9 %copy.13 = bf16[64,4096]{1,0:T(8,128)(2,1)} copy(bf16[64,4096]{1,0:T(8,128)(2,1)} %shard_map.109) | data formatting | bytes 1048576

commit v6 on v5

--- a/solution.py
+++ b/solution.py
@@ -250,6 +250,13 @@
         to_ring(k).start()
         return 0
 
+    active = jnp.transpose(jnp.where(near_list[...] >= 0, 1.0, 0.0))
+    lists = jnp.concatenate([active[:, 0:9], active[:, 9:18], active[:, 18:27]], axis=0).astype(BF16)
+    blocked = jnp.where(mm(pick[...], lists) > 0.5, 0.0, jnp.inf)
+    low2 = lax.broadcasted_iota(jnp.int32, (128, 128), 1) < 64
+    for j in range(9):
+        masks[j] = jnp.where(low2, blocked[0:128, j : j + 1], blocked[128:256, j : j + 1])
+
     pl.semaphore_wait(barrier, COLS - 1 + 7 + 5)
     for k in (1, 2, 3):
         to_quad(k).start()
@@ -260,13 +267,6 @@
     one_all[COLS] = jnp.zeros((4, 32, 128), BF16)
     two_all[r] = two_send[...]
     two_all[ROWS] = jnp.zeros((16, 128), BF16)
-
-    active = jnp.transpose(jnp.where(near_list[...] >= 0, 1.0, 0.0))
-    lists = jnp.concatenate([active[:, 0:9], active[:, 9:18], active[:, 18:27]], axis=0).astype(BF16)
-    blocked = jnp.where(mm(pick[...], lists) > 0.5, 0.0, jnp.inf)
-    low2 = lax.broadcasted_iota(jnp.int32, (128, 128), 1) < 64
-    for j in range(9):
-        masks[j] = jnp.where(low2, blocked[0:128, j : j + 1], blocked[128:256, j : j + 1])
 
     coord = lax.broadcasted_iota(jnp.int32, (4, 256), 0)
     middle = jnp.where(coord == 0, 4 * c + 2, jnp.where(coord == 1, 4 * r + 2, jnp.where(coord == 2, 2, 0))).astype(F32)
@@ -290,15 +290,23 @@
         wide_c[e, :, 384:512] = jnp.concatenate([zero, c0[:, 64:]], axis=1)
         return p, size
 
+    at_row = lax.rem(lax.broadcasted_iota(jnp.int32, (32, 512), 0), 8)
+    at_lane = lax.broadcasted_iota(jnp.int32, (32, 512), 1) // 128
+    spread = jnp.where(at_row == at_lane, 1.0, 0.0).astype(BF16)
+
     def own_column(i, _):
         x, y = i // 4, lax.rem(i, 4)
         p, size = prepare(1 + y, 1 + x)
-        features = (p[0:1], p[1:2], p[2:3], size + SOFT)
-        for f, row in enumerate(features):
-            for h in range(2):
-                half = jnp.broadcast_to(row[:, h * 128 : h * 128 + 128], (128, 128))
-                own_f[i, f, h * 128 : h * 128 + 128] = jnp.transpose(half)
-            own_f[i, f, 256:320] = jnp.where(low, own_f[i, f, 64:128], own_f[i, f, 128:192])
+        whole = jnp.concatenate([p[0:3], size + SOFT, jnp.zeros((4, 256), F32)], axis=0)
+        first = whole.astype(BF16).astype(F32)
+        rest = whole - first
+        second = rest.astype(BF16).astype(F32)
+        parts = jnp.concatenate([first, second, rest - second, jnp.zeros((8, 256), F32)], axis=0).astype(BF16)
+        wide = mm(parts, spread, TN)
+        for f in range(4):
+            w = wide[:, f * 128 : f * 128 + 128]
+            own_f[i, f, 0:256] = w
+            own_f[i, f, 256:320] = jnp.where(low, w[64:128], w[128:192])
         return 0
 
     lax.fori_loop(0, 16, own_column, 0, unroll=2)
@@ -348,7 +356,7 @@
             along(k, *gather).start()
     for copy in x_halo:
         copy.start()
-    lax.fori_loop(0, 4, unit_step, 0)
+    lax.fori_loop(0, 4, unit_step, 0, unroll=4)
 
     for copy in y_halo:
         copy.wait()
@@ -359,7 +367,7 @@
         return 0
 
     lax.fori_loop(0, 4, beside_y, 0, unroll=True)
-    lax.fori_loop(4, 8, unit_step, 0)
+    lax.fori_loop(4, 8, unit_step, 0, unroll=4)
 
     def wait_ring(k, _):
         to_ring(k).wait()
@@ -425,7 +433,7 @@
         return 0
 
     lax.fori_loop(0, 4, beside_x, 0, unroll=True)
-    lax.fori_loop(8, 12, unit_step, 0)
+    lax.fori_loop(8, 12, unit_step, 0, unroll=4)
 
     def wait_part(k, _):
         part_copy(k).wait()
@@ -469,7 +477,7 @@
     for y in (0, 5):
         for x in (0, 5):
             prepare(y, x)
-    lax.fori_loop(12, 16, unit_step, 0)
+    lax.fori_loop(12, 16, unit_step, 0, unroll=4)
     lax.fori_loop(0, 8, finish, 0, unroll=True)
 
 

time: 42.7 us -> 41.4 us (0.970)
  Pallas kernels: 40.7 us -> 39.2 us
    pallas_call x1, Pallas kernels: 40.7 us -> 39.2 us  [shards(): pl.pallas_call(body, out_shape=jax.ShapeDtypeStruct(charges.shape, BF16),...]
where the time goes in v6:
time: 41.4 us; the launch traced here: 41.1 us
  Pallas kernels  39.2 us (95%)
  local copies, waits for them, and re-layouts  1.87 us (5%)
    pallas_call x1, Pallas kernels, shards(): pl.pallas_call(body, out_shape=jax.ShapeDtypeStruct(charges.shape, BF16),...  39.2 us
    unnamed x1, local copies, waits for them, and re-layouts  1.87 us

profile of v6, /device:TPU:1, one launch (start us, length us, event | category | flops | bytes accessed | tf_op | source)
XLA Modules:
  0.0 41.1 jit_solution(4135199984991507467)
XLA Ops:
  0.0 39.2 %shard_map.109 = bf16[64,4096]{1,0:T(8,128)(2,1)} custom-call(bf16[64,4096]{1,0:T(8,128)(2,1)} %charges.1, f32[3,4096]{1,0:T(4,128)} %points.1, bf16[32,4096]{1,0:T(8,128)(2,1)} %basis.1, bf16[1024,64]{1,0:T(8,128)(2,1)} %bitcast.6, bf16[256,32]{1,0:T(8,128)(2,1)} %bitcast.8, bf16[8,12,32,32]{3,2,1,0:T(8,128)(2,1)} %c_one.1, bf16[16,32,32]{2,1,0:T(8,128)(2,1)} %bitcast.7, ...), custom_call_target="tpu_custom_call" | custom-call | tf_op jit(solution)/shard_map/pallas_call | solution.py:488
  39.2 1.9 %copy.13 = bf16[64,4096]{1,0:T(8,128)(2,1)} copy(bf16[64,4096]{1,0:T(8,128)(2,1)} %shard_map.109) | data formatting | bytes 1048576

commit v7 on v6

--- a/solution.py
+++ b/solution.py
@@ -347,6 +347,8 @@
         unit(i)
         return 0
 
+    for copy in x_halo:
+        copy.start()
     for k in (1, 2, 3):
         to_quad(k).wait()
     lax.fori_loop(1, 8, start_ring, 0)
@@ -354,8 +356,6 @@
         across(*gather).wait()
         for k in (1, 2, 3):
             along(k, *gather).start()
-    for copy in x_halo:
-        copy.start()
     lax.fori_loop(0, 4, unit_step, 0, unroll=4)
 
     for copy in y_halo:

time: 41.4 us -> 44.1 us (1.065)
  Pallas kernels: 39.2 us -> 42 us
    pallas_call x1, Pallas kernels: 39.2 us -> 42 us  [shards(): pl.pallas_call(body, out_shape=jax.ShapeDtypeStruct(charges.shape, BF16),...]
where the time goes in v7:
time: 44.1 us; the launch traced here: 43.9 us
  Pallas kernels  42 us (95%)
  local copies, waits for them, and re-layouts  1.87 us (4%)
    pallas_call x1, Pallas kernels, shards(): pl.pallas_call(body, out_shape=jax.ShapeDtypeStruct(charges.shape, BF16),...  42 us
    unnamed x1, local copies, waits for them, and re-layouts  1.87 us

profile of v7, /device:TPU:1, one launch (start us, length us, event | category | flops | bytes accessed | tf_op | source)
XLA Modules:
  0.0 43.9 jit_solution(3302182116076070679)
XLA Ops:
  0.0 42.0 %shard_map.109 = bf16[64,4096]{1,0:T(8,128)(2,1)} custom-call(bf16[64,4096]{1,0:T(8,128)(2,1)} %charges.1, f32[3,4096]{1,0:T(4,128)} %points.1, bf16[32,4096]{1,0:T(8,128)(2,1)} %basis.1, bf16[1024,64]{1,0:T(8,128)(2,1)} %bitcast.6, bf16[256,32]{1,0:T(8,128)(2,1)} %bitcast.8, bf16[8,12,32,32]{3,2,1,0:T(8,128)(2,1)} %c_one.1, bf16[16,32,32]{2,1,0:T(8,128)(2,1)} %bitcast.7, ...), custom_call_target="tpu_custom_call" | custom-call | tf_op jit(solution)/shard_map/pallas_call | solution.py:488
  42.1 1.9 %copy.13 = bf16[64,4096]{1,0:T(8,128)(2,1)} copy(bf16[64,4096]{1,0:T(8,128)(2,1)} %shard_map.109) | data formatting | bytes 1048576
